TPU v7x, 512 devices: a whole 4x4x16 slice. The times are simulated.
512 devices in a mesh: dp: 8 (over y, core), row: 8 (over z_lo), col: 8 (over z_hi, x).
Axes of the slice: x: 4, y: 4, z: 16 (z_hi: 2, z_lo: 8; z = z_hi * 8 + z_lo), core: 2. Of those that a mesh axis runs over, the one named last changes fastest.
Arguments:
- queries: bfloat16 [8, 1024, 8192], P('dp', 'row', 'col'), may hold values from -6 to 6
- keys_in: bfloat16 [8, 1024, 8192], P('dp', 'row', 'col'), may hold values from -6 to 6
- values_in: bfloat16 [8, 1024, 8192], P('dp', 'row', 'col'), may hold values from -6 to 6
- out_weight: bfloat16 [8, 8, 128, 6144], P(None, 'row', None, 'col'), may hold values from -0.0625 to 0.0625
- out_grad: bfloat16 [8, 1024, 6144], P('dp', 'row', 'col'), may hold values from -4 to 4
Outputs:
- projected: bfloat16 [8, 1024, 6144], P('dp', 'row', 'col')
- grad_queries: bfloat16 [8, 1024, 8192], P('dp', 'row', 'col')
- grad_keys: bfloat16 [8, 1024, 8192], P('dp', 'row', 'col')
- grad_values: bfloat16 [8, 1024, 8192], P('dp', 'row', 'col')
- grad_weight: bfloat16 [8, 8, 128, 6144], P(None, 'row', None, 'col')
All inputs are finite; a program needn't handle non-finite values.
Results may differ from a plain program's by a relative error of at most 0.034.
Values may be sent and summed in bfloat16 or wider, within the bound.
No kernel may reach another device: no remote copies, remote signals or barrier semaphores. Data moves between devices by JAX's collectives and lax.ppermute only.
A program may use at most 64 MiB of HBM per device.

v0:
```python
import math

import jax
import jax.numpy as jnp
from jax import lax
from jax.sharding import PartitionSpec as P

HEAD_DIM = 128


def weight_gradient(head_rows, grad_all, weight_shape):
    local_sum = lax.dot_general(
        head_rows, grad_all, (((0,), (0,)), ((), ())), preferred_element_type=jnp.float32
    )
    summed = lax.psum(local_sum.astype(jnp.bfloat16), "dp")
    return summed.reshape(weight_shape)


def body(queries, keys_in, values_in, out_weight, out_grad):
    tok_rows = queries.shape[1]
    col_width = queries.shape[2]
    row_devices = lax.axis_size("row")
    seq_len = tok_rows * row_devices
    heads_here = col_width // row_devices // HEAD_DIM
    score_scale = 1.0 / math.sqrt(HEAD_DIM)
    query_heads, key_heads, value_heads = (
        lax.all_to_all(queries[0], "row", split_axis=1, concat_axis=0, tiled=True),
        lax.all_to_all(keys_in[0], "row", split_axis=1, concat_axis=0, tiled=True),
        lax.all_to_all(values_in[0], "row", split_axis=1, concat_axis=0, tiled=True),
    )
    query_cube = query_heads.reshape(seq_len, heads_here, HEAD_DIM)
    key_cube = key_heads.reshape(seq_len, heads_here, HEAD_DIM)
    value_cube = value_heads.reshape(seq_len, heads_here, HEAD_DIM)
    span_rows = min(seq_len, 512)
    span_count = seq_len // span_rows
    positions = jnp.arange(seq_len, dtype=jnp.int32)
    span_starts = jnp.arange(span_count, dtype=jnp.int32) * span_rows

    def probabilities(first_row):
        query_rows = lax.dynamic_slice_in_dim(query_cube, first_row, span_rows, 0)
        scores = (
            jnp.einsum("qhd,khd->hqk", query_rows, key_cube, preferred_element_type=jnp.float32)
            * score_scale
        )
        query_pos = first_row + jnp.arange(span_rows, dtype=jnp.int32)
        causal = positions[None, None, :] <= query_pos[None, :, None]
        scores = jnp.where(causal, scores, jnp.float32(-1e30))
        row_max = jnp.max(scores, axis=-1, keepdims=True)
        expo = jnp.exp(scores - row_max)
        return (expo / jnp.sum(expo, axis=-1, keepdims=True), query_rows)

    def forward_span(first_row):
        prob_matrix, query_rows = probabilities(first_row)
        return jnp.einsum(
            "hqk,khd->qhd",
            prob_matrix.astype(jnp.bfloat16),
            value_cube,
            preferred_element_type=jnp.float32,
        ).astype(jnp.bfloat16)

    head_out = lax.map(forward_span, span_starts).reshape(seq_len, heads_here * HEAD_DIM)
    head_rows = lax.all_gather(head_out, "col", axis=1, tiled=True)
    weight_rows = out_weight.reshape(-1, out_weight.shape[3])
    panel = head_rows
    projected = lax.psum_scatter(
        jnp.dot(panel, weight_rows, preferred_element_type=jnp.float32).astype(jnp.bfloat16),
        "row",
        scatter_dimension=0,
        tiled=True,
    )
    grad_all = lax.all_gather(out_grad[0], "row", axis=0, tiled=True)
    panel = weight_rows
    head_grad_t = lax.psum_scatter(
        jnp.einsum("xd,td->xt", panel, grad_all, preferred_element_type=jnp.float32).astype(
            jnp.bfloat16
        ),
        "col",
        scatter_dimension=0,
        tiled=True,
    )
    grad_cube = head_grad_t.reshape(heads_here, HEAD_DIM, seq_len)

    def backward_span(sums, first_row):
        key_sum, value_sum = sums
        prob_matrix, query_rows = probabilities(first_row)
        prob_half = prob_matrix.astype(jnp.bfloat16)
        grad_span = lax.dynamic_slice_in_dim(grad_cube, first_row, span_rows, 2)
        dprobs = jnp.einsum(
            "heq,khe->hqk", grad_span, value_cube, preferred_element_type=jnp.float32
        )
        row_dot = jnp.sum(prob_matrix * dprobs, axis=-1, keepdims=True)
        dscores = (prob_matrix * (dprobs - row_dot)).astype(jnp.bfloat16)
        query_grad = (
            jnp.einsum("hqk,khe->qhe", dscores, key_cube, preferred_element_type=jnp.float32)
            * score_scale
        ).astype(jnp.bfloat16)
        key_sum = key_sum + jnp.einsum(
            "hqk,qhe->khe", dscores, query_rows, preferred_element_type=jnp.float32
        )
        value_sum = value_sum + jnp.einsum(
            "hqk,heq->khe", prob_half, grad_span, preferred_element_type=jnp.float32
        )
        return ((key_sum, value_sum), query_grad)

    empty_sum = jnp.zeros((seq_len, heads_here, HEAD_DIM), jnp.float32)
    (key_sum, value_sum), query_spans = lax.scan(backward_span, (empty_sum, empty_sum), span_starts)
    query_back = query_spans.reshape(seq_len, heads_here * HEAD_DIM)
    key_back = (key_sum * score_scale).astype(jnp.bfloat16).reshape(seq_len, heads_here * HEAD_DIM)
    value_back = value_sum.astype(jnp.bfloat16).reshape(seq_len, heads_here * HEAD_DIM)
    grad_q, grad_k, grad_v = (
        lax.all_to_all(query_back, "row", split_axis=0, concat_axis=1, tiled=True),
        lax.all_to_all(key_back, "row", split_axis=0, concat_axis=1, tiled=True),
        lax.all_to_all(value_back, "row", split_axis=0, concat_axis=1, tiled=True),
    )
    grad_weight = weight_gradient(head_rows, grad_all, out_weight.shape)
    return (projected[None], grad_q[None], grad_k[None], grad_v[None], grad_weight)


def solution(mesh):
    placed = (
        P("dp", "row", "col"),
        P("dp", "row", "col"),
        P("dp", "row", "col"),
        P(None, "row", None, "col"),
        P("dp", "row", "col"),
    )
    return jax.shard_map(
        body,
        mesh=mesh,
        in_specs=placed,
        out_specs=(
            P("dp", "row", "col"),
            P("dp", "row", "col"),
            P("dp", "row", "col"),
            P("dp", "row", "col"),
            P(None, "row", None, "col"),
        ),
        check_vma=False,
    )
```

profile of v0, /device:TPU:4, one launch (start us, length us, event | category | flops | bytes accessed | tf_op | source)
XLA Modules:
  0.0 552.4 jit_solution(8026849421882415293)
XLA Ops:
  7.2 1.9 copy.40
  9.1 12.5 %all-to-all-start = ((bf16[128,8,128]{0,2,1:T(8,128)(2,1)}), bf16[128,8,128]{0,2,1:T(8,128)(2,1)S(1)}, u32[]{:S(2)}, u32[]{:S(2)}) async-start(bf16[128,8,128]{0,2,1:T(8,128)(2,1)} %bitcast), calls=%async_computation | async-start | bytes 524288 | tf_op jit(solution)/shard_map/all_to_all | solution.py:27
  23.4 14.9 %all-to-all-done = bf16[128,8,128]{0,2,1:T(8,128)(2,1)S(1)} async-done(((bf16[128,8,128]{0,2,1:T(8,128)(2,1)}), bf16[128,8,128]{0,2,1:T(8,128)(2,1)S(1)}, u32[]{:S(2)}, u32[]{:S(2)}) %all-to-all-start) | async-done | bytes 262176 | tf_op jit(solution)/shard_map/all_to_all | solution.py:27
  38.3 5.1 all-to-all-start.1
  44.2 15.4 %all-to-all-done.1 = bf16[128,8,128]{0,2,1:T(8,128)(2,1)S(1)} async-done(((bf16[128,8,128]{0,2,1:T(8,128)(2,1)}), bf16[128,8,128]{0,2,1:T(8,128)(2,1)S(1)}, u32[]{:S(2)}, u32[]{:S(2)}) %all-to-all-start.1) | async-done | bytes 262176 | tf_op jit(solution)/shard_map/all_to_all | solution.py:28
  59.7 5.1 all-to-all-start.2
  65.9 15.1 %all-to-all-done.2 = bf16[128,8,128]{0,2,1:T(8,128)(2,1)S(1)} async-done(((bf16[128,8,128]{0,2,1:T(8,128)(2,1)}), bf16[128,8,128]{0,2,1:T(8,128)(2,1)S(1)}, u32[]{:S(2)}, u32[]{:S(2)}) %all-to-all-start.2) | async-done | bytes 262176 | tf_op jit(solution)/shard_map/all_to_all | solution.py:29
  81.2 9.9 %while.26 = (s32[]{:T(128)}, bf16[2,512,1,128]{3,1,2,0:T(8,128)(2,1)S(1)}, s32[2]{0:T(128)S(1)}, bf16[1024,1,128]{2,0,1:T(8,128)(2,1)S(1)}, bf16[1024,1,128]{2,0...) while((s32[]{:T(128)}, ...), condition=%wide.region_3.4_spmd.clone, body=%wide.region_0.3_spmd.clone.sunk | while | flops 273219072 | bytes 7092375 | solution.py:61
  91.8 44.6 %all-gather.6.cloned.1.call-done = bf16[1,1024,768]{2,1,0:T(8,128)(2,1)} async-done(((bf16[1,128,768]{2,1,0:T(8,128)(2,1)}), bf16[1,1024,768]{2,1,0:T(8,128)(2,1)}) %all-gather.6.cloned.1.call-update) | async-done | bytes 1572880 | tf_op jit(solution)/shard_map/all_gather | solution.py:71
  136.5 4.5 convolution_convert_fusion.1
  141.1 111.9 %all-gather.4.cloned.1.call-done = bf16[1024,1024]{1,0:T(8,128)(2,1)} async-done(((bf16[1024,128]{1,0:T(8,128)(2,1)}), bf16[1024,1024]{1,0:T(8,128)(2,1)}) %all-gather.4.cloned.1.call-update) | async-done | bytes 2097168 | tf_op jit(solution)/shard_map/all_gather | solution.py:62
  253.0 5.1 convolution_convert_fusion.2
  258.2 4.5 convolution_convert_fusion.3
  262.7 132.7 %reduce-scatter.5.cloned.1.call-done = bf16[128,1024]{1,0:T(8,128)(2,1)} async-done(((bf16[1024,1024]{1,0:T(8,128)(2,1)}), bf16[128,1024]{1,0:T(8,128)(2,1)}) %reduce-scatter.5.cloned.1.call-update) | async-done | bytes 262160 | tf_op jit(solution)/shard_map/reduce_scatter | solution.py:73
  396.2 22.4 %while.27 = (s32[]{:T(128)}, f32[1024,1,128]{0,2,1:T(8,128)S(1)}, f32[1024,1,128]{0,2,1:T(8,128)S(1)}, bf16[2,512,1,128]{3,1,2,0:T(8,128)(2,1)}, s32[2]{0:T(128)...) while((s32[]{:T(128)}, f32[1024,1,128]{0,2,1:T(8,128)S(1)}, ...), condition=%wide.region_10.11_spmd.clone, body=%wide.region_6.10_spmd.clone.sunk | while | flops 681180160 | bytes 39217940 | solution.py:106
  401.8 2.5 fusion.75
  413.1 2.5 fusion.75
  419.5 3.4 all-to-all-start.4
  423.2 15.5 %all-to-all-done.4 = bf16[8,128,128]{2,1,0:T(8,128)(2,1)S(1)} async-done(((bf16[8,128,128]{2,1,0:T(8,128)(2,1)}), bf16[8,128,128]{2,1,0:T(8,128)(2,1)S(1)}, u32[]{:S(2)}, u32[]{:S(2)}) %all-to-all-start.4) | async-done | bytes 262176 | tf_op jit(solution)/shard_map/all_to_all | solution.py:112
  438.7 21.1 %all_to_all.96 = bf16[8,128,128]{2,1,0:T(8,128)(2,1)S(1)} all-to-all(bf16[8,128,128]{2,1,0:T(8,128)(2,1)S(1)} %bitcast.155), channel_id=1, replica_groups=mesh['dp'=8,'row'=8,'col'=8] {'row'}, dimensions={0} | all-to-all | bytes 524288 | tf_op jit(solution)/shard_map/all_to_all | solution.py:113
  459.8 5.1 all-to-all-start.3
  466.9 14.2 %all-to-all-done.3 = bf16[8,128,128]{2,1,0:T(8,128)(2,1)S(1)} async-done(((bf16[8,128,128]{2,1,0:T(8,128)(2,1)}), bf16[8,128,128]{2,1,0:T(8,128)(2,1)S(1)}, u32[]{:S(2)}, u32[]{:S(2)}) %all-to-all-start.3) | async-done | bytes 262176 | tf_op jit(solution)/shard_map/all_to_all | solution.py:111
  482.2 61.0 %reduce-scatter.3.cloned.1.call-done = bf16[128,768]{1,0:T(8,128)(2,1)} async-done(((bf16[1024,768]{1,0:T(8,128)(2,1)}), bf16[128,768]{1,0:T(8,128)(2,1)}) %reduce-scatter.3.cloned.1.call-update) | async-done | bytes 196624 | tf_op jit(solution)/shard_map/reduce_scatter | solution.py:65
  543.2 2.7 copy.76
  (75 shorter events, 29.1 us)
Async XLA Ops:
  7.2 129.3 %copy-start = (bf16[8,1,128,768]{3,2,1,0:T(8,128)(2,1)S(1)}, bf16[8,1,128,768]{3,2,1,0:T(8,128)(2,1)}, u32[]{:S(2)}) copy-start(bf16[8,1,128,768]{3,2,1,0:T(8,128)(2,1)} %param.12) | copy-start | bytes 4718596
  7.2 36.2 %copy-start.4 = (bf16[1,128,1024]{2,1,0:T(8,128)(2,1)S(1)}, bf16[1,128,1024]{2,1,0:T(8,128)(2,1)}, u32[]{:S(2)}) copy-start(bf16[1,128,1024]{2,1,0:T(8,128)(2,1)} %param.11) | copy-start | bytes 786436
  9.1 29.2 %all-to-all-start = ((bf16[128,8,128]{0,2,1:T(8,128)(2,1)}), bf16[128,8,128]{0,2,1:T(8,128)(2,1)S(1)}, u32[]{:S(2)}, u32[]{:S(2)}) async-start(bf16[128,8,128]{0,2,1:T(8,128)(2,1)} %bitcast), calls=%async_computation | async-start | bytes 524288 | tf_op jit(solution)/shard_map/all_to_all | solution.py:27
  38.3 21.3 %all-to-all-start.1 = ((bf16[128,8,128]{0,2,1:T(8,128)(2,1)}), bf16[128,8,128]{0,2,1:T(8,128)(2,1)S(1)}, u32[]{:S(2)}, u32[]{:S(2)}) async-start(bf16[128,8,128]{0,2,1:T(8,128)(2,1)} %bitcast.3), calls=%async_computation.1 | async-start | bytes 524288 | tf_op jit(solution)/shard_map/all_to_all | solution.py:28
  59.7 21.3 %all-to-all-start.2 = ((bf16[128,8,128]{0,2,1:T(8,128)(2,1)}), bf16[128,8,128]{0,2,1:T(8,128)(2,1)S(1)}, u32[]{:S(2)}, u32[]{:S(2)}) async-start(bf16[128,8,128]{0,2,1:T(8,128)(2,1)} %bitcast.6), calls=%async_computation.2 | async-start | bytes 524288 | tf_op jit(solution)/shard_map/all_to_all | solution.py:29
  64.7 71.8 %all-gather.6.cloned.1.call-start = ((), (), s32[]{:S(2)}) async-start(), calls=%async_computation.12 | async-start | bytes 1769472 | tf_op jit(solution)/shard_map/all_gather | solution.py:71
  65.5 187.6 %all-gather.4.cloned.1.call-start = ((), (), s32[]{:S(2)}) async-start(), calls=%async_computation.8 | async-start | bytes 2359296 | tf_op jit(solution)/shard_map/all_gather | solution.py:62
  91.1 0.7 copy-start.3
  91.8 303.7 %reduce-scatter.5.cloned.1.call-start = ((), (), s32[]{:S(2)}) async-start(), calls=%async_computation.10 | async-start | bytes 2359296 | tf_op jit(solution)/shard_map/reduce_scatter | solution.py:73
  141.1 341.1 %all-reduce.2.cloned.1.call-start = ((), (), s32[]{:S(2)}) async-start(), calls=%async_computation.11 | async-start | bytes 3145728 | tf_op jit(solution)/shard_map/psum | solution.py:15
  258.1 285.1 %reduce-scatter.3.cloned.1.call-start = ((), (), s32[]{:S(2)}) async-start(), calls=%async_computation.9 | async-start | bytes 1769472 | tf_op jit(solution)/shard_map/reduce_scatter | solution.py:65
  400.0 1.3 copy-start.1
  401.8 2.6 copy-start.2
  401.8 2.6 copy-start.5
  411.2 1.3 copy-start.1
  413.0 2.6 copy-start.2
  413.1 2.6 copy-start.5
  419.5 19.1 %all-to-all-start.4 = ((bf16[8,128,128]{2,1,0:T(8,128)(2,1)}), bf16[8,128,128]{2,1,0:T(8,128)(2,1)S(1)}, u32[]{:S(2)}, u32[]{:S(2)}) async-start(bf16[8,128,128]{2,1,0:T(8,128)(2,1)} %bitcast.17), calls=%async_computation.6 | async-start | bytes 524288 | tf_op jit(solution)/shard_map/all_to_all | solution.py:112
  459.8 21.3 %all-to-all-start.3 = ((bf16[8,128,128]{2,1,0:T(8,128)(2,1)}), bf16[8,128,128]{2,1,0:T(8,128)(2,1)S(1)}, u32[]{:S(2)}, u32[]{:S(2)}) async-start(bf16[8,128,128]{2,1,0:T(8,128)(2,1)} %bitcast.14), calls=%async_computation.5 | async-start | bytes 524288 | tf_op jit(solution)/shard_map/all_to_all | solution.py:111
Sparse Core Ops, SparseCore 0:
  67.6 68.8 all-gather.5
  140.1 112.8 all-gather.3
  257.7 137.7 reduce-scatter.4
  397.8 72.2 all-reduce.1
  473.6 69.5 reduce-scatter.2
where the time goes:
time: 553 us; the launch traced here: 552 us
  waiting for transfers between devices  426 us (77%)
  starting transfers between devices  31.3 us (6%)
  matrix products  27.7 us (5%)
  blocking collectives  21.1 us (4%)
  local copies, waits for them, and re-layouts  18.3 us (3%)
  between operations  13.9 us (3%)
  loops' own time  7.97 us (1%)
  other arithmetic  5.83 us (1%)
    reduce_scatter x1, waiting for transfers between devices, body(): lax.psum_scatter(jnp.einsum('xd,td->xt', panel, grad_all, preferred_eleme...  133 us
    all_gather x1, waiting for transfers between devices, body(): head_rows = lax.all_gather(head_out, 'col', axis=1, tiled=True)  112 us
    reduce_scatter x1, waiting for transfers between devices, body(): lax.psum_scatter(jnp.dot(panel, weight_rows, preferred_element_type=jnp.f...  61 us
    all_gather x1, waiting for transfers between devices, body(): grad_all = lax.all_gather(out_grad[0], 'row', axis=0, tiled=True)  44.6 us
    all_to_all x1, blocking collectives, body(): lax.all_to_all(value_back, 'row', split_axis=0, concat_axis=1, tiled=True)  21.1 us
    all_to_all x1, waiting for transfers between devices, body(): lax.all_to_all(key_back, 'row', split_axis=0, concat_axis=1, tiled=True)  15.5 us
    all_to_all x1, waiting for transfers between devices, body(): lax.all_to_all(keys_in[0], 'row', split_axis=1, concat_axis=0, tiled=True)  15.4 us
    all_to_all x1, waiting for transfers between devices, body(): lax.all_to_all(values_in[0], 'row', split_axis=1, concat_axis=0, tiled=True)  15.1 us
  transfers between devices with their start and end apart: 10, of which 9 were waited for; matrix products, arithmetic and copies ran while one was open for 8% of the time, Pallas kernels for 0%

commit v1 on v0

v1 whole, which is shorter than its diff:
```python
import math

import jax
import jax.numpy as jnp
from jax import lax
from jax.sharding import Mesh, PartitionSpec as P

HEAD_DIM = 128
DP = ("y", "core")
ROW = "row"
COL = ("zhi", "x")
RING = ("zhi", "row")
F32 = jnp.float32
BF16 = jnp.bfloat16


def attention_forward(query, key, value):
    seq_len = query.shape[0]
    scale = 1.0 / math.sqrt(HEAD_DIM)
    scores = lax.dot_general(query, key, (((1,), (1,)), ((), ())), preferred_element_type=F32) * scale
    positions = jnp.arange(seq_len, dtype=jnp.int32)
    causal = positions[None, :] <= positions[:, None]
    scores = jnp.where(causal, scores, F32(-1e30))
    row_max = jnp.max(scores, axis=-1, keepdims=True)
    expo = jnp.exp(scores - row_max)
    probs = expo / jnp.sum(expo, axis=-1, keepdims=True)
    head_out = jnp.dot(probs.astype(BF16), value, preferred_element_type=F32).astype(BF16)
    return head_out, probs


def attention_backward(query, key, value, probs, grad):
    scale = 1.0 / math.sqrt(HEAD_DIM)
    dprobs = lax.dot_general(grad, value, (((1,), (1,)), ((), ())), preferred_element_type=F32)
    row_dot = jnp.sum(probs * dprobs, axis=-1, keepdims=True)
    dscores = (probs * (dprobs - row_dot)).astype(BF16)
    d_query = (jnp.dot(dscores, key, preferred_element_type=F32) * scale).astype(BF16)
    over_rows = (((0,), (0,)), ((), ()))
    d_key = (lax.dot_general(dscores, query, over_rows, preferred_element_type=F32) * scale).astype(BF16)
    d_value = lax.dot_general(probs.astype(BF16), grad, over_rows, preferred_element_type=F32).astype(BF16)
    return d_query, d_key, d_value


def shifts(count):
    return [[(i, (i + d) % count) for i in range(count)] for d in range(1, count)]


def body(queries, keys_in, values_in, out_weight, out_grad):
    tok = queries.shape[1]
    n_row = lax.axis_size("row")
    n_x = lax.axis_size("x")
    n_dp = lax.axis_size("y") * lax.axis_size("core")
    seq_len = tok * n_row
    width = out_grad.shape[2]
    zhi = lax.axis_index("zhi")
    dp = lax.axis_index("y") * lax.axis_size("core") + lax.axis_index("core")
    swap = [(0, 1), (1, 0)]

    with jax.named_scope("grad_gather"):
        grad_all = lax.all_gather(out_grad[0], RING, axis=0, tiled=True).reshape(2, seq_len, width)

    with jax.named_scope("qkv_exchange"):
        by_head = lambda a: a[0].reshape(tok, n_row, HEAD_DIM).transpose(1, 0, 2)
        stacked = jnp.stack([by_head(queries), by_head(keys_in), by_head(values_in)], axis=1)
        heads = lax.all_to_all(stacked, ROW, 0, 0, tiled=True)
        query, key, value = (heads[:, i].reshape(seq_len, HEAD_DIM) for i in range(3))

    with jax.named_scope("weight_swap"):
        w_rows = out_weight.reshape(-1, width)
        half = w_rows.shape[0] // 2
        piece = half // n_dp
        away = lax.dynamic_slice_in_dim(w_rows, (1 - zhi) * half + dp * piece, piece, 0)
        arrived = lax.ppermute(away, "zhi", swap)
        w_other = lax.all_gather(arrived, DP, axis=0, tiled=True)
        w_own = lax.dynamic_slice_in_dim(w_rows, zhi * half, half, 0)
        first = zhi == 0
        w0 = jnp.where(first, w_own, w_other)
        w1 = jnp.where(first, w_other, w_own)

    with jax.named_scope("attend"):
        head_out, probs = attention_forward(query, key, value)

    with jax.named_scope("head_gather"):
        x_index = lax.axis_index("x")
        got = [head_out] + [lax.ppermute(head_out, "x", s) for s in shifts(n_x)]
        ordered = jnp.stack(got)
        heads_x = jnp.concatenate(
            [lax.dynamic_index_in_dim(ordered, (x_index - i) % n_x, 0, keepdims=False) for i in range(n_x)], axis=1
        )

    with jax.named_scope("head_grad"):
        over_n = (((1,), (1,)), ((), ()))
        hg = lax.dot_general(grad_all[0], w0, over_n, preferred_element_type=F32)
        hg = hg + lax.dot_general(grad_all[1], w1, over_n, preferred_element_type=F32)
        hg = hg.astype(BF16).reshape(seq_len, n_x, HEAD_DIM).transpose(1, 0, 2)
        hg = lax.all_to_all(hg, "x", 0, 0, tiled=True)
        grad = jnp.sum(hg.astype(F32), axis=0).astype(BF16)

    with jax.named_scope("project"):
        part0 = jnp.dot(heads_x, w0, preferred_element_type=F32).astype(BF16)
        part1 = jnp.dot(heads_x, w1, preferred_element_type=F32).astype(BF16)
        parts = jnp.concatenate([part0, part1], axis=0)
        projected = lax.psum_scatter(parts, RING, scatter_dimension=0, tiled=True)

    with jax.named_scope("weight_grad"):
        over_t = (((0,), (0,)), ((), ()))
        dw = [
            lax.dot_general(heads_x, grad_all[i], over_t, preferred_element_type=F32).astype(BF16) for i in range(2)
        ]
        dw = jnp.stack([m.reshape(n_dp, piece, width) for m in dw], axis=1)
        dw = lax.all_to_all(dw, DP, 0, 0, tiled=True)
        dw = jnp.sum(dw.astype(F32), axis=0).astype(BF16)
        dw_own = lax.dynamic_index_in_dim(dw, zhi, 0, keepdims=False)
        dw_away = lax.dynamic_index_in_dim(dw, 1 - zhi, 0, keepdims=False)
        dw_back = lax.ppermute(dw_away, "zhi", swap)
        own_rows = lax.all_gather(dw_own, DP, axis=0, tiled=True)
        other_rows = lax.all_gather(dw_back, DP, axis=0, tiled=True)
        grad_weight = jnp.concatenate(
            [jnp.where(first, own_rows, other_rows), jnp.where(first, other_rows, own_rows)], axis=0
        ).reshape(out_weight.shape)

    with jax.named_scope("attend_back"):
        grads = attention_backward(query, key, value, probs, grad)

    with jax.named_scope("qkv_return"):
        back = jnp.stack([g.reshape(n_row, tok, HEAD_DIM) for g in grads], axis=1)
        back = lax.all_to_all(back, ROW, 0, 0, tiled=True)
        outs = [back[:, i].transpose(1, 0, 2).reshape(1, tok, n_row * HEAD_DIM) for i in range(3)]
    return (projected[None], *outs, grad_weight)


def solution(mesh):
    fine = Mesh(mesh.devices.reshape(4, 2, 8, 2, 4), ("y", "core", "row", "zhi", "x"))
    act = P(DP, ROW, COL)
    wgt = P(None, ROW, None, COL)
    return jax.shard_map(
        body,
        mesh=fine,
        in_specs=(act, act, act, wgt, act),
        out_specs=(act, act, act, act, wgt),
        check_vma=False,
    )
```

time: 553 us -> 253 us (0.46)
  the two profiles are of different devices: /device:TPU:4 before, /device:TPU:65 now
where the time goes in v1:
time: 253 us; the launch traced here: 252 us
  waiting for transfers between devices  96.4 us (38%)
  starting transfers between devices  59.6 us (24%)
  blocking collectives  46.1 us (18%)
  matrix products  17.5 us (7%)
  between operations  14.4 us (6%)
  local copies, waits for them, and re-layouts  10.3 us (4%)
  other arithmetic  7.72 us (3%)
    all_to_all x1, waiting for transfers between devices, body(): heads = lax.all_to_all(stacked, ROW, 0, 0, tiled=True)  36 us
    ppermute x1, waiting for transfers between devices, body(): dw_back = lax.ppermute(dw_away, 'zhi', swap)  33.3 us
    all_gather x1, blocking collectives, body(): w_other = lax.all_gather(arrived, DP, axis=0, tiled=True)  17.2 us
    all_gather x1, blocking collectives, body(): own_rows = lax.all_gather(dw_own, DP, axis=0, tiled=True)  15 us
    all_gather x1, blocking collectives, body(): other_rows = lax.all_gather(dw_back, DP, axis=0, tiled=True)  13.9 us
    all_to_all x1, starting transfers between devices, body(): dw = lax.all_to_all(dw, DP, 0, 0, tiled=True)  13.6 us
    all_to_all x1, waiting for transfers between devices, body(): dw = lax.all_to_all(dw, DP, 0, 0, tiled=True)  12.7 us
    all_to_all x1, starting transfers between devices, body(): heads = lax.all_to_all(stacked, ROW, 0, 0, tiled=True)  11.6 us
  transfers between devices with their start and end apart: 11, of which 5 were waited for; matrix products, arithmetic and copies ran while one was open for 12% of the time, Pallas kernels for 0%

profile of v1, /device:TPU:65, one launch (start us, length us, event | category | flops | bytes accessed | tf_op | source)
XLA Modules:
  0.0 252.0 jit_solution(16349625201101293727)
XLA Ops:
  11.6 11.6 %all-to-all-start = ((bf16[8,3,128,128]{2,3,1,0:T(8,128)(2,1)}), bf16[8,3,128,128]{2,3,1,0:T(8,128)(2,1)S(1)}, u32[]{:S(2)}, u32[]{:S(2)}) async-start(bf16[8,3,128,128]{2,3,1,0:T(8,128)(2,1)} %copy.40), calls=%async_computation | async-start | bytes 1572864 | tf_op jit(solution)/shard_map/qkv_exchange/all_to_all | solution.py:64
  24.9 7.9 %collective-permute-start.3 = (bf16[64,768]{1,0:T(8,128)(2,1)S(1)}, bf16[64,768]{1,0:T(8,128)(2,1)S(1)}, u32[]{:S(2)}, u32[]{:S(2)}) collective-permute-start(bf16[64,768]{1,0:T(8,128)(2,1)S(1)} %constant_dynamic-slice_fusion.1), channel_id=1, source_target_pairs={{0,4},{4,0},{1,5},{5,1},{2,6},{6,2},{3,7},{7,3},{8,12},{12,8},{9,1... | collective-permute-start | bytes 294920 | tf_op jit(solution)/shard_map/weight_swap/ppermute | solution.py:72
  32.9 36.0 %all-to-all-done = bf16[8,3,128,128]{2,3,1,0:T(8,128)(2,1)S(1)} async-done(((bf16[8,3,128,128]{2,3,1,0:T(8,128)(2,1)}), bf16[8,3,128,128]{2,3,1,0:T(8,128)(2,1)S(1)}, u32[]{:S(2)}, u32[]{:S(2)}) %all-to-all-start) | async-done | bytes 786464 | tf_op jit(solution)/shard_map/qkv_exchange/all_to_all | solution.py:64
  72.3 4.5 %collective-permute-start.2 = (bf16[1024,128]{0,1:T(8,128)(2,1)S(1)}, bf16[1024,128]{0,1:T(8,128)(2,1)S(1)}, u32[]{:S(2)}, u32[]{:S(2)}) collective-permute-start(bf16[1024,128]{0,1:T(8,128)(2,1)S(1)} %convolution_convert_fusion.5), channel_id=1, source_target_pairs={{0,3},{1,0},{2,1},{3,2},{4,7},{5,4},{6,5},{7,6},{8,11},{9,8},{10,9... | collective-permute-start | bytes 786440 | tf_op jit(solution)/shard_map/head_gather/ppermute | solution.py:84
  76.8 2.4 collective-permute-start.1
  79.2 2.5 collective-permute-start
  81.8 17.2 %all_gather.12 = bf16[512,768]{1,0:T(8,128)(2,1)S(1)} all-gather(bf16[64,768]{1,0:T(8,128)(2,1)S(1)} %collective-permute-done.3), channel_id=1, replica_groups=mesh['y'=4,'core'=2,'row'=8,'zhi'=2,'x'=4] {'y','core'}, dimensions={0}, use_global_device_ids=true | all-gather | bytes 884736 | tf_op jit(solution)/shard_map/weight_swap/all_gather | solution.py:73
  101.3 1.9 pad_maximum_fusion
  103.2 8.8 %all-gather.4.cloned.1.call-done = bf16[1,2048,768]{2,1,0:T(8,128)(2,1)} async-done(((bf16[1,128,768]{2,1,0:T(8,128)(2,1)}), bf16[1,2048,768]{2,1,0:T(8,128)(2,1)}) %all-gather.4.cloned.1.call-update) | async-done | bytes 3145744 | tf_op jit(solution)/shard_map/grad_gather/all_gather | solution.py:59
  112.0 2.8 %fusion.3 = f32[512,1024]{1,0:T(8,128)S(1)} fusion(bf16[1,2048,768]{2,1,0:T(8,128)(2,1)} %all-gather.4.cloned.1.call-done, bf16[512,768]{1,0:T(8,128)(2,1)S(1)} %all_gather.12, pred[]{:T(512)S(6)} %eq.8, bf16[1024,768]{1,0:T(8,128)(2,1)} %bitcast.114, s32[]{:T(128)S(6)} %select_n.79), kind=kOutput, calls=%fused_computation.18 | convolution fusion | flops 805699584 | bytes 5242885 | tf_op jit(solution)/shard_map/head_grad/dot_general | solution.py:93
  115.1 2.0 add_convert_fusion
  117.1 3.7 %all-to-all-start.1 = ((bf16[4,1024,128]{1,2,0:T(8,128)(2,1)}), bf16[4,1024,128]{1,2,0:T(8,128)(2,1)S(1)}, u32[]{:S(2)}, u32[]{:S(2)}) async-start(bf16[4,1024,128]{1,2,0:T(8,128)(2,1)} %bitcast.26), calls=%async_computation.2 | async-start | bytes 2097152 | tf_op jit(solution)/shard_map/head_grad/all_to_all | solution.py:95
  120.8 2.5 %convolution_convert_fusion.3 = bf16[512,768]{1,0:T(8,128)(2,1)S(1)} fusion(bf16[1,2048,768]{2,1,0:T(8,128)(2,1)} %all-gather.4.cloned.1.call-done, bf16[1024,128]{0,1:T(8,128)(2,1)S(1)} %get-tuple-element.13, bf16[1024,128]{0,1:T(8,128)(2,1)S(1)} %get-tuple-element.14, bf16[1024,128]{0,1:T(8,128)(2,1)S(1)} %get-tuple-element.15, ...), kind=kOutput, calls=%fused_computation.17 | convolution fusion | flops 809893888 | bytes 3407872 | tf_op jit(solution)/shard_map/weight_grad/dot_general | solution.py:107
  124.4 1.3 pad_maximum_fusion.1
  125.7 4.9 %all-to-all-done.1 = bf16[4,1024,128]{1,2,0:T(8,128)(2,1)S(1)} async-done(((bf16[4,1024,128]{1,2,0:T(8,128)(2,1)}), bf16[4,1024,128]{1,2,0:T(8,128)(2,1)S(1)}, u32[]{:S(2)}, u32[]{:S(2)}) %all-to-all-start.1) | async-done | bytes 1048608 | tf_op jit(solution)/shard_map/head_grad/all_to_all | solution.py:95
  130.6 13.6 %all-to-all-start.3 = ((bf16[8,2,64,768]{3,2,1,0:T(8,128)(2,1)}), bf16[8,2,64,768]{3,2,1,0:T(8,128)(2,1)S(1)}, u32[]{:S(2)}, u32[]{:S(2)}) async-start(bf16[8,2,64,768]{3,2,1,0:T(8,128)(2,1)} %pad_maximum_fusion.1), calls=%async_computation.4 | async-start | bytes 3145728 | tf_op jit(solution)/shard_map/weight_grad/all_to_all | solution.py:110
  144.4 3.3 %multiply_reduce_fusion = (f32[1024]{0:T(1024)S(1)}, f32[1024,1024]{0,1:T(8,128)S(1)}) fusion(f32[1024]{0:T(1024)S(1)} %fusion.1, f32[1024]{0:T(1024)S(1)} %get-tuple-element.24, f32[1024,1024]{0,1:T(8,128)} %copy-done, bf16[1024,128]{1,0:T(8,128)(2,1)} %bitcast.105, bf16[1024,128]{0,1:T(8,128)(2,1)S(1)} %reduce_sum.43), kind=kOutput, calls=%fused_computation.1 | convolution fusion | flops 275774464 | bytes 8925184 | tf_op jit(solution)/shard_map/attend_back/dot_general | solution.py:33
  152.3 12.7 %all-to-all-done.3 = bf16[8,2,64,768]{3,2,1,0:T(8,128)(2,1)S(1)} async-done(((bf16[8,2,64,768]{3,2,1,0:T(8,128)(2,1)}), bf16[8,2,64,768]{3,2,1,0:T(8,128)(2,1)S(1)}, u32[]{:S(2)}, u32[]{:S(2)}) %all-to-all-start.3) | async-done | bytes 1572896 | tf_op jit(solution)/shard_map/weight_grad/all_to_all | solution.py:110
  164.9 6.6 %all-to-all-start.2 = ((bf16[8,3,128,128]{3,2,1,0:T(8,128)(2,1)}), bf16[8,3,128,128]{3,2,1,0:T(8,128)(2,1)S(1)}, u32[]{:S(2)}, u32[]{:S(2)}) async-start(bf16[8,3,128,128]{3,2,1,0:T(8,128)(2,1)} %pad_maximum_fusion.6), calls=%async_computation.3 | async-start | bytes 1572864 | tf_op jit(solution)/shard_map/qkv_return/all_to_all | solution.py:126
  171.8 6.6 %collective-permute-start.4 = (bf16[64,768]{1,0:T(8,128)(2,1)S(1)}, bf16[64,768]{1,0:T(8,128)(2,1)S(1)}, u32[]{:S(2)}, u32[]{:S(2)}) collective-permute-start(bf16[64,768]{1,0:T(8,128)(2,1)S(1)} %get-tuple-element.23), channel_id=1, source_target_pairs={{0,4},{4,0},{1,5},{5,1},{2,6},{6,2},{3,7},{7,3},{8,12},{12,8},{9,1... | collective-permute-start | bytes 294920 | tf_op jit(solution)/shard_map/weight_grad/ppermute | solution.py:114
  178.4 15.0 %all-gather.1 = bf16[1,512,768]{2,1,0:T(8,128)(2,1)S(1)} all-gather(bf16[1,64,768]{2,1,0:T(8,128)(2,1)S(1)} %get-tuple-element.22), channel_id=3, replica_groups=mesh['y'=4,'core'=2,'row'=8,'zhi'=2,'x'=4] {'y','core'}, dimensions={1}, use_global_device_ids=true | all-gather | bytes 884736 | tf_op jit(solution)/shard_map/weight_grad/all_gather | solution.py:115
  193.4 33.3 %collective-permute-done.4 = bf16[64,768]{1,0:T(8,128)(2,1)S(1)} collective-permute-done((bf16[64,768]{1,0:T(8,128)(2,1)S(1)}, bf16[64,768]{1,0:T(8,128)(2,1)S(1)}, u32[]{:S(2)}, u32[]{:S(2)}) %collective-permute-start.4) | collective-permute-done | bytes 98336 | tf_op jit(solution)/shard_map/weight_grad/ppermute | solution.py:114
  226.7 13.9 %all_gather.15 = bf16[512,768]{1,0:T(8,128)(2,1)S(1)} all-gather(bf16[64,768]{1,0:T(8,128)(2,1)S(1)} %collective-permute-done.4), channel_id=1, replica_groups=mesh['y'=4,'core'=2,'row'=8,'zhi'=2,'x'=4] {'y','core'}, dimensions={0}, use_global_device_ids=true | all-gather | bytes 884736 | tf_op jit(solution)/shard_map/weight_grad/all_gather | solution.py:116
  240.7 1.2 pad_maximum_fusion.2
  (58 shorter events, 21.1 us)
Async XLA Ops:
  11.6 57.4 %all-to-all-start = ((bf16[8,3,128,128]{2,3,1,0:T(8,128)(2,1)}), bf16[8,3,128,128]{2,3,1,0:T(8,128)(2,1)S(1)}, u32[]{:S(2)}, u32[]{:S(2)}) async-start(bf16[8,3,128,128]{2,3,1,0:T(8,128)(2,1)} %copy.40), calls=%async_computation | async-start | bytes 1572864 | tf_op jit(solution)/shard_map/qkv_exchange/all_to_all | solution.py:64
  23.2 88.8 %all-gather.4.cloned.1.call-start = ((), (), s32[]{:S(2)}) async-start(), calls=%async_computation.6 | async-start | bytes 3342336 | tf_op jit(solution)/shard_map/grad_gather/all_gather | solution.py:59
  23.9 221.2 %reduce-scatter.2.cloned.1.call-start = ((), (), s32[]{:S(2)}) async-start(), calls=%async_computation.5 | async-start | bytes 3342336 | tf_op jit(solution)/shard_map/project/reduce_scatter | solution.py:102
  24.9 56.9 %collective-permute-start.3 = (bf16[64,768]{1,0:T(8,128)(2,1)S(1)}, bf16[64,768]{1,0:T(8,128)(2,1)S(1)}, u32[]{:S(2)}, u32[]{:S(2)}) collective-permute-start(bf16[64,768]{1,0:T(8,128)(2,1)S(1)} %constant_dynamic-slice_fusion.1), channel_id=1, source_target_pairs={{0,4},{4,0},{1,5},{5,1},{2,6},{6,2},{3,7},{7,3},{8,12},{12,8},{9,1... | collective-permute-start | bytes 294920 | tf_op jit(solution)/shard_map/weight_swap/ppermute | solution.py:72
  69.6 1.3 copy-start.2
  70.3 2.0 copy-start
  72.3 26.9 %copy-start.3 = (bf16[8,1,128,768]{3,2,1,0:T(8,128)(2,1)S(1)}, bf16[8,1,128,768]{3,2,1,0:T(8,128)(2,1)}, u32[]{:S(2)}) copy-start(bf16[8,1,128,768]{3,2,1,0:T(8,128)(2,1)} %param.8) | copy-start | bytes 4718596
  72.3 26.7 %collective-permute-start.2 = (bf16[1024,128]{0,1:T(8,128)(2,1)S(1)}, bf16[1024,128]{0,1:T(8,128)(2,1)S(1)}, u32[]{:S(2)}, u32[]{:S(2)}) collective-permute-start(bf16[1024,128]{0,1:T(8,128)(2,1)S(1)} %convolution_convert_fusion.5), channel_id=1, source_target_pairs={{0,3},{1,0},{2,1},{3,2},{4,7},{5,4},{6,5},{7,6},{8,11},{9,8},{10,9... | collective-permute-start | bytes 786440 | tf_op jit(solution)/shard_map/head_gather/ppermute | solution.py:84
  76.8 22.2 %collective-permute-start.1 = (bf16[1024,128]{0,1:T(8,128)(2,1)S(1)}, bf16[1024,128]{0,1:T(8,128)(2,1)S(1)}, u32[]{:S(2)}, u32[]{:S(2)}) collective-permute-start(bf16[1024,128]{0,1:T(8,128)(2,1)S(1)} %convolution_convert_fusion.5), channel_id=1, source_target_pairs={{0,2},{1,3},{2,0},{3,1},{4,6},{5,7},{6,4},{7,5},{8,10},{9,11},{10,... | collective-permute-start | bytes 786440 | tf_op jit(solution)/shard_map/head_gather/ppermute | solution.py:84
  79.2 19.7 %collective-permute-start = (bf16[1024,128]{0,1:T(8,128)(2,1)S(1)}, bf16[1024,128]{0,1:T(8,128)(2,1)S(1)}, u32[]{:S(2)}, u32[]{:S(2)}) collective-permute-start(bf16[1024,128]{0,1:T(8,128)(2,1)S(1)} %convolution_convert_fusion.5), channel_id=1, source_target_pairs={{0,1},{1,2},{2,3},{3,0},{4,5},{5,6},{6,7},{7,4},{8,9},{9,10},{10,1... | collective-permute-start | bytes 786440 | tf_op jit(solution)/shard_map/head_gather/ppermute | solution.py:84
  112.0 2.8 %copy-start.4 = (bf16[8,1,128,768]{3,2,1,0:T(8,128)(2,1)S(1)}, bf16[8,1,128,768]{3,2,1,0:T(8,128)(2,1)}, u32[]{:S(2)}) copy-start(bf16[8,1,128,768]{3,2,1,0:T(8,128)(2,1)} %param.8) | copy-start | bytes 4718596
  112.0 3.1 %copy-start.5 = (bf16[1,2048,768]{2,1,0:T(8,128)(2,1)S(1)}, bf16[1,2048,768]{2,1,0:T(8,128)(2,1)}, u32[]{:S(2)}) copy-start(bf16[1,2048,768]{2,1,0:T(8,128)(2,1)} %all-gather.4.cloned.1.call-done) | copy-start | bytes 9437188
  117.1 13.5 %all-to-all-start.1 = ((bf16[4,1024,128]{1,2,0:T(8,128)(2,1)}), bf16[4,1024,128]{1,2,0:T(8,128)(2,1)S(1)}, u32[]{:S(2)}, u32[]{:S(2)}) async-start(bf16[4,1024,128]{1,2,0:T(8,128)(2,1)} %bitcast.26), calls=%async_computation.2 | async-start | bytes 2097152 | tf_op jit(solution)/shard_map/head_grad/all_to_all | solution.py:95
  120.8 2.6 %copy-start.6 = (bf16[1,2048,768]{2,1,0:T(8,128)(2,1)S(1)}, bf16[1,2048,768]{2,1,0:T(8,128)(2,1)}, u32[]{:S(2)}) copy-start(bf16[1,2048,768]{2,1,0:T(8,128)(2,1)} %all-gather.4.cloned.1.call-done) | copy-start | bytes 9437188
  130.6 34.4 %all-to-all-start.3 = ((bf16[8,2,64,768]{3,2,1,0:T(8,128)(2,1)}), bf16[8,2,64,768]{3,2,1,0:T(8,128)(2,1)S(1)}, u32[]{:S(2)}, u32[]{:S(2)}) async-start(bf16[8,2,64,768]{3,2,1,0:T(8,128)(2,1)} %pad_maximum_fusion.1), calls=%async_computation.4 | async-start | bytes 3145728 | tf_op jit(solution)/shard_map/weight_grad/all_to_all | solution.py:110
  144.4 3.6 %copy-start.1 = (f32[1024,1024]{0,1:T(8,128)S(1)}, f32[1024,1024]{0,1:T(8,128)}, u32[]{:S(2)}) copy-start(f32[1024,1024]{0,1:T(8,128)} %copy-done) | copy-start | bytes 12582916
  164.9 77.0 %all-to-all-start.2 = ((bf16[8,3,128,128]{3,2,1,0:T(8,128)(2,1)}), bf16[8,3,128,128]{3,2,1,0:T(8,128)(2,1)S(1)}, u32[]{:S(2)}, u32[]{:S(2)}) async-start(bf16[8,3,128,128]{3,2,1,0:T(8,128)(2,1)} %pad_maximum_fusion.6), calls=%async_computation.3 | async-start | bytes 1572864 | tf_op jit(solution)/shard_map/qkv_return/all_to_all | solution.py:126
  171.8 54.9 %collective-permute-start.4 = (bf16[64,768]{1,0:T(8,128)(2,1)S(1)}, bf16[64,768]{1,0:T(8,128)(2,1)S(1)}, u32[]{:S(2)}, u32[]{:S(2)}) collective-permute-start(bf16[64,768]{1,0:T(8,128)(2,1)S(1)} %get-tuple-element.23), channel_id=1, source_target_pairs={{0,4},{4,0},{1,5},{5,1},{2,6},{6,2},{3,7},{7,3},{8,12},{12,8},{9,1... | collective-permute-start | bytes 294920 | tf_op jit(solution)/shard_map/weight_grad/ppermute | solution.py:114
Sparse Core Ops, SparseCore 0:
  26.1 85.8 all-gather.3
  115.4 99.9 reduce-scatter.1

commit v2 on v1

--- a/solution.py
+++ b/solution.py
@@ -44,6 +44,21 @@
     return [[(i, (i + d) % count) for i in range(count)] for d in range(1, count)]
 
 
+def reduce_scatter_dp(blocks, piece):
+    n_y, n_core = lax.axis_size("y"), lax.axis_size("core")
+    y, core = lax.axis_index("y"), lax.axis_index("core")
+    width = blocks[0].shape[1]
+    cut = jnp.stack([b.reshape(n_y, n_core, piece, width) for b in blocks], axis=2)
+    mine = lax.dynamic_index_in_dim(cut, core, 1, keepdims=False)
+    away = lax.dynamic_index_in_dim(cut, 1 - core, 1, keepdims=False)
+    mine = (mine.astype(F32) + lax.ppermute(away, "core", [(0, 1), (1, 0)]).astype(F32)).astype(BF16)
+    total = lax.dynamic_index_in_dim(mine, y, 0, keepdims=False).astype(F32)
+    for d, pairs in enumerate(shifts(n_y), 1):
+        sent = lax.dynamic_index_in_dim(mine, (y + d) % n_y, 0, keepdims=False)
+        total = total + lax.ppermute(sent, "y", pairs).astype(F32)
+    return total.astype(BF16)
+
+
 def body(queries, keys_in, values_in, out_weight, out_grad):
     tok = queries.shape[1]
     n_row = lax.axis_size("row")
@@ -87,6 +102,14 @@
             [lax.dynamic_index_in_dim(ordered, (x_index - i) % n_x, 0, keepdims=False) for i in range(n_x)], axis=1
         )
 
+    with jax.named_scope("project"):
+        part0 = jnp.dot(heads_x, w0, preferred_element_type=F32).astype(BF16)
+        part1 = jnp.dot(heads_x, w1, preferred_element_type=F32).astype(BF16)
+        part0, part1, grad_all = lax.optimization_barrier((part0, part1, grad_all))
+        parts = jnp.concatenate([part0, part1], axis=0)
+        parts, grad_all = lax.optimization_barrier((parts, grad_all))
+        projected = lax.psum_scatter(parts, RING, scatter_dimension=0, tiled=True)
+
     with jax.named_scope("head_grad"):
         over_n = (((1,), (1,)), ((), ()))
         hg = lax.dot_general(grad_all[0], w0, over_n, preferred_element_type=F32)
@@ -95,20 +118,12 @@
         hg = lax.all_to_all(hg, "x", 0, 0, tiled=True)
         grad = jnp.sum(hg.astype(F32), axis=0).astype(BF16)
 
-    with jax.named_scope("project"):
-        part0 = jnp.dot(heads_x, w0, preferred_element_type=F32).astype(BF16)
-        part1 = jnp.dot(heads_x, w1, preferred_element_type=F32).astype(BF16)
-        parts = jnp.concatenate([part0, part1], axis=0)
-        projected = lax.psum_scatter(parts, RING, scatter_dimension=0, tiled=True)
-
     with jax.named_scope("weight_grad"):
         over_t = (((0,), (0,)), ((), ()))
         dw = [
             lax.dot_general(heads_x, grad_all[i], over_t, preferred_element_type=F32).astype(BF16) for i in range(2)
         ]
-        dw = jnp.stack([m.reshape(n_dp, piece, width) for m in dw], axis=1)
-        dw = lax.all_to_all(dw, DP, 0, 0, tiled=True)
-        dw = jnp.sum(dw.astype(F32), axis=0).astype(BF16)
+        dw = reduce_scatter_dp(dw, piece)
         dw_own = lax.dynamic_index_in_dim(dw, zhi, 0, keepdims=False)
         dw_away = lax.dynamic_index_in_dim(dw, 1 - zhi, 0, keepdims=False)
         dw_back = lax.ppermute(dw_away, "zhi", swap)

time: 253 us -> 240 us (0.949)
  the two profiles are of different devices: /device:TPU:65 before, /device:TPU:12 now
where the time goes in v2:
time: 240 us; the launch traced here: 239 us
  waiting for transfers between devices  85.6 us (36%)
  starting transfers between devices  60.7 us (25%)
  blocking collectives  40.2 us (17%)
  matrix products  17.3 us (7%)
  between operations  14.6 us (6%)
  local copies, waits for them, and re-layouts  12 us (5%)
  other arithmetic  8.38 us (3%)
    all_to_all x1, waiting for transfers between devices, body(): heads = lax.all_to_all(stacked, ROW, 0, 0, tiled=True)  45.2 us
    reduce_scatter x1, waiting for transfers between devices, body(): projected = lax.psum_scatter(parts, RING, scatter_dimension=0, tiled=True)  20.8 us
    all_gather x1, blocking collectives, body(): w_other = lax.all_gather(arrived, DP, axis=0, tiled=True)  13.7 us
    all_gather x1, blocking collectives, body(): other_rows = lax.all_gather(dw_back, DP, axis=0, tiled=True)  13.4 us
    all_gather x1, blocking collectives, body(): own_rows = lax.all_gather(dw_own, DP, axis=0, tiled=True)  13.2 us
    all_to_all x1, starting transfers between devices, body(): heads = lax.all_to_all(stacked, ROW, 0, 0, tiled=True)  12.5 us
    all_gather x1, waiting for transfers between devices, body(): lax.all_gather(out_grad[0], RING, axis=0, tiled=True)  12 us
    ppermute x3, starting transfers between devices, reduce_scatter_dp(): total = total + lax.ppermute(sent, 'y', pairs).astype(F32)  10.6 us
  transfers between devices with their start and end apart: 14, of which 7 were waited for; matrix products, arithmetic and copies ran while one was open for 14% of the time, Pallas kernels for 0%

profile of v2, /device:TPU:12, one launch (start us, length us, event | category | flops | bytes accessed | tf_op | source)
XLA Modules:
  0.0 238.9 jit_solution(3329634826969708431)
XLA Ops:
  12.3 12.5 %all-to-all-start = ((bf16[8,3,128,128]{2,3,1,0:T(8,128)(2,1)}), bf16[8,3,128,128]{2,3,1,0:T(8,128)(2,1)S(1)}, u32[]{:S(2)}, u32[]{:S(2)}) async-start(bf16[8,3,128,128]{2,3,1,0:T(8,128)(2,1)} %copy.38), calls=%async_computation | async-start | bytes 1572864 | tf_op jit(solution)/shard_map/qkv_exchange/all_to_all | solution.py:79
  25.8 8.2 %collective-permute-start.3 = (bf16[64,768]{1,0:T(8,128)(2,1)S(1)}, bf16[64,768]{1,0:T(8,128)(2,1)S(1)}, u32[]{:S(2)}, u32[]{:S(2)}) collective-permute-start(bf16[64,768]{1,0:T(8,128)(2,1)S(1)} %constant_dynamic-slice_fusion.1), channel_id=1, source_target_pairs={{0,4},{4,0},{1,5},{5,1},{2,6},{6,2},{3,7},{7,3},{8,12},{12,8},{9,1... | collective-permute-start | bytes 294920 | tf_op jit(solution)/shard_map/weight_swap/ppermute | solution.py:87
  34.1 45.2 %all-to-all-done = bf16[8,3,128,128]{2,3,1,0:T(8,128)(2,1)S(1)} async-done(((bf16[8,3,128,128]{2,3,1,0:T(8,128)(2,1)}), bf16[8,3,128,128]{2,3,1,0:T(8,128)(2,1)S(1)}, u32[]{:S(2)}, u32[]{:S(2)}) %all-to-all-start) | async-done | bytes 786464 | tf_op jit(solution)/shard_map/qkv_exchange/all_to_all | solution.py:79
  82.7 2.6 %collective-permute-start.2 = (bf16[1024,128]{0,1:T(8,128)(2,1)S(1)}, bf16[1024,128]{0,1:T(8,128)(2,1)S(1)}, u32[]{:S(2)}, u32[]{:S(2)}) collective-permute-start(bf16[1024,128]{0,1:T(8,128)(2,1)S(1)} %convolution_convert_fusion.3), channel_id=1, source_target_pairs={{0,3},{1,0},{2,1},{3,2},{4,7},{5,4},{6,5},{7,6},{8,11},{9,8},{10,9... | collective-permute-start | bytes 786440 | tf_op jit(solution)/shard_map/head_gather/ppermute | solution.py:99
  85.2 4.7 %collective-permute-start.1 = (bf16[1024,128]{0,1:T(8,128)(2,1)S(1)}, bf16[1024,128]{0,1:T(8,128)(2,1)S(1)}, u32[]{:S(2)}, u32[]{:S(2)}) collective-permute-start(bf16[1024,128]{0,1:T(8,128)(2,1)S(1)} %convolution_convert_fusion.3), channel_id=1, source_target_pairs={{0,2},{1,3},{2,0},{3,1},{4,6},{5,7},{6,4},{7,5},{8,10},{9,11},{10,... | collective-permute-start | bytes 786440 | tf_op jit(solution)/shard_map/head_gather/ppermute | solution.py:99
  91.8 13.7 %all_gather.12 = bf16[512,768]{1,0:T(8,128)(2,1)S(1)} all-gather(bf16[64,768]{1,0:T(8,128)(2,1)S(1)} %collective-permute-done.3), channel_id=1, replica_groups=mesh['y'=4,'core'=2,'row'=8,'zhi'=2,'x'=4] {'y','core'}, dimensions={0}, use_global_device_ids=true | all-gather | bytes 884736 | tf_op jit(solution)/shard_map/weight_swap/all_gather | solution.py:88
  108.0 12.0 %all-gather.4.cloned.1.call-done = bf16[1,2048,768]{2,1,0:T(8,128)(2,1)} async-done(((bf16[1,128,768]{2,1,0:T(8,128)(2,1)}), bf16[1,2048,768]{2,1,0:T(8,128)(2,1)}) %all-gather.4.cloned.1.call-update) | async-done | bytes 3145744 | tf_op jit(solution)/shard_map/grad_gather/all_gather | solution.py:74
  123.5 2.6 %fusion.6 = f32[1024,512]{0,1:T(8,128)S(1)} fusion(bf16[2,1024,768]{2,1,0:T(8,128)(2,1)} %bitcast.137, bf16[512,768]{1,0:T(8,128)(2,1)S(1)} %copy-done.3, pred[]{:T(512)S(6)} %eq.11, bf16[1024,768]{1,0:T(8,128)(2,1)S(1)} %bitcast.135, s32[]{:T(128)S(6)} %select_n.111), kind=kOutput, calls=%fused_computation.21 | convolution fusion | flops 805699584 | bytes 5242885 | tf_op jit(solution)/shard_map/head_grad/dot_general | solution.py:116
  126.4 2.0 add_convert_fusion
  128.4 4.8 %all-to-all-start.1 = ((bf16[4,1024,128]{1,2,0:T(8,128)(2,1)}), bf16[4,1024,128]{1,2,0:T(8,128)(2,1)S(1)}, u32[]{:S(2)}, u32[]{:S(2)}) async-start(bf16[4,1024,128]{1,2,0:T(8,128)(2,1)} %bitcast.26), calls=%async_computation.2 | async-start | bytes 2097152 | tf_op jit(solution)/shard_map/head_grad/all_to_all | solution.py:118
  133.2 2.5 %fusion.11 = bf16[512,768]{1,0:T(8,128)(2,1)S(1)} fusion(bf16[2,1024,768]{2,1,0:T(8,128)(2,1)} %bitcast.138, bf16[1024,128]{0,1:T(8,128)(2,1)S(1)} %copy-done.5, bf16[1024,128]{0,1:T(8,128)(2,1)S(1)} %copy-done.7, bf16[1024,128]{0,1:T(8,128)(2,1)S(1)} %copy-done.9, bf16[1024,128]{0,1:T(8,128)(2,1)S(1)} %get-tuple-element.22), kind=kOutput, calls=%fused_computation.26 | convolution fusion | flops 809893888 | bytes 3407872 | tf_op jit(solution)/shard_map/weight_grad/dot_general | solution.py:124
  136.9 2.1 collective-permute-start.4
  139.0 2.1 all-to-all-done.1
  142.1 3.4 %multiply_reduce_fusion = (f32[1024]{0:T(1024)S(1)}, f32[1024,1024]{0,1:T(8,128)S(1)}) fusion(f32[1024]{0:T(1024)S(1)} %fusion.1, f32[1024]{0:T(1024)S(1)} %get-tuple-element.37, f32[1024,1024]{0,1:T(8,128)} %copy-done, bf16[1024,128]{1,0:T(8,128)(2,1)} %bitcast.124, bf16[1024,128]{0,1:T(8,128)(2,1)} %reduce_sum.31), kind=kOutput, calls=%fused_computation.1 | convolution fusion | flops 275774464 | bytes 8925184 | tf_op jit(solution)/shard_map/attend_back/dot_general | solution.py:33
  150.0 6.0 %all-to-all-start.2 = ((bf16[8,3,128,128]{3,2,1,0:T(8,128)(2,1)}), bf16[8,3,128,128]{3,2,1,0:T(8,128)(2,1)S(1)}, u32[]{:S(2)}, u32[]{:S(2)}) async-start(bf16[8,3,128,128]{3,2,1,0:T(8,128)(2,1)} %pad_maximum_fusion.5), calls=%async_computation.3 | async-start | bytes 1572864 | tf_op jit(solution)/shard_map/qkv_return/all_to_all | solution.py:141
  157.4 2.4 %collective-permute-start.7 = (bf16[2,64,768]{2,1,0:T(8,128)(2,1)S(1)}, bf16[2,64,768]{2,1,0:T(8,128)(2,1)S(1)}, u32[]{:S(2)}, u32[]{:S(2)}) collective-permute-start(bf16[2,64,768]{2,1,0:T(8,128)(2,1)S(1)} %get-tuple-element.27), channel_id=1, source_target_pairs={{0,384},{128,0},{256,128},{384,256},{1,385},{129,1},{257,129},{385... | collective-permute-start | bytes 589832 | tf_op jit(solution)/shard_map/weight_grad/ppermute | solution.py:58
  159.8 4.4 %collective-permute-start.6 = (bf16[2,64,768]{2,1,0:T(8,128)(2,1)S(1)}, bf16[2,64,768]{2,1,0:T(8,128)(2,1)S(1)}, u32[]{:S(2)}, u32[]{:S(2)}) collective-permute-start(bf16[2,64,768]{2,1,0:T(8,128)(2,1)S(1)} %get-tuple-element.28), channel_id=1, source_target_pairs={{0,256},{128,384},{256,0},{384,128},{1,257},{129,385},{257,1},{385... | collective-permute-start | bytes 589832 | tf_op jit(solution)/shard_map/weight_grad/ppermute | solution.py:58
  164.3 3.7 %collective-permute-start.5 = (bf16[2,64,768]{2,1,0:T(8,128)(2,1)S(1)}, bf16[2,64,768]{2,1,0:T(8,128)(2,1)S(1)}, u32[]{:S(2)}, u32[]{:S(2)}) collective-permute-start(bf16[2,64,768]{2,1,0:T(8,128)(2,1)S(1)} %get-tuple-element.26), channel_id=1, source_target_pairs={{0,128},{128,256},{256,384},{384,0},{1,129},{129,257},{257,385},{3... | collective-permute-start | bytes 589832 | tf_op jit(solution)/shard_map/weight_grad/ppermute | solution.py:58
  168.0 2.0 collective-permute-done.6
  169.9 2.6 %collective-permute-done.5 = bf16[2,64,768]{2,1,0:T(8,128)(2,1)S(1)} collective-permute-done((bf16[2,64,768]{2,1,0:T(8,128)(2,1)S(1)}, bf16[2,64,768]{2,1,0:T(8,128)(2,1)S(1)}, u32[]{:S(2)}, u32[]{:S(2)}) %collective-permute-start.5) | collective-permute-done | bytes 196640 | tf_op jit(solution)/shard_map/weight_grad/ppermute | solution.py:58
  172.7 7.3 %collective-permute-start.8 = (bf16[64,768]{1,0:T(8,128)(2,1)S(1)}, bf16[64,768]{1,0:T(8,128)(2,1)S(1)}, u32[]{:S(2)}, u32[]{:S(2)}) collective-permute-start(bf16[64,768]{1,0:T(8,128)(2,1)S(1)} %get-tuple-element.36), channel_id=1, source_target_pairs={{0,4},{4,0},{1,5},{5,1},{2,6},{6,2},{3,7},{7,3},{8,12},{12,8},{9,1... | collective-permute-start | bytes 294920 | tf_op jit(solution)/shard_map/weight_grad/ppermute | solution.py:129
  180.0 13.2 %all-gather.1 = bf16[1,512,768]{2,1,0:T(8,128)(2,1)S(1)} all-gather(bf16[1,64,768]{2,1,0:T(8,128)(2,1)S(1)} %get-tuple-element.35), channel_id=3, replica_groups=mesh['y'=4,'core'=2,'row'=8,'zhi'=2,'x'=4] {'y','core'}, dimensions={1}, use_global_device_ids=true | all-gather | bytes 884736 | tf_op jit(solution)/shard_map/weight_grad/all_gather | solution.py:130
  193.2 13.4 %all_gather.15 = bf16[512,768]{1,0:T(8,128)(2,1)S(1)} all-gather(bf16[64,768]{1,0:T(8,128)(2,1)S(1)} %collective-permute-done.8), channel_id=1, replica_groups=mesh['y'=4,'core'=2,'row'=8,'zhi'=2,'x'=4] {'y','core'}, dimensions={0}, use_global_device_ids=true | all-gather | bytes 884736 | tf_op jit(solution)/shard_map/weight_grad/all_gather | solution.py:131
  211.3 20.8 %reduce-scatter.2.cloned.1.call-done = bf16[128,768]{1,0:T(8,128)(2,1)} async-done(((bf16[2048,768]{1,0:T(8,128)(2,1)}), bf16[128,768]{1,0:T(8,128)(2,1)}) %reduce-scatter.2.cloned.1.call-update) | async-done | bytes 196624 | tf_op jit(solution)/shard_map/project/reduce_scatter | solution.py:111
  (96 shorter events, 30.1 us)
Async XLA Ops:
  7.2 112.8 %all-gather.4.cloned.1.call-start = ((), (), s32[]{:S(2)}) async-start(), calls=%async_computation.5 | async-start | bytes 3342336 | tf_op jit(solution)/shard_map/grad_gather/all_gather | solution.py:74
  12.3 67.0 %all-to-all-start = ((bf16[8,3,128,128]{2,3,1,0:T(8,128)(2,1)}), bf16[8,3,128,128]{2,3,1,0:T(8,128)(2,1)S(1)}, u32[]{:S(2)}, u32[]{:S(2)}) async-start(bf16[8,3,128,128]{2,3,1,0:T(8,128)(2,1)} %copy.38), calls=%async_computation | async-start | bytes 1572864 | tf_op jit(solution)/shard_map/qkv_exchange/all_to_all | solution.py:79
  24.9 207.2 %reduce-scatter.2.cloned.1.call-start = ((), (), s32[]{:S(2)}) async-start(), calls=%async_computation.4 | async-start | bytes 3342336 | tf_op jit(solution)/shard_map/project/reduce_scatter | solution.py:111
  25.8 66.0 %collective-permute-start.3 = (bf16[64,768]{1,0:T(8,128)(2,1)S(1)}, bf16[64,768]{1,0:T(8,128)(2,1)S(1)}, u32[]{:S(2)}, u32[]{:S(2)}) collective-permute-start(bf16[64,768]{1,0:T(8,128)(2,1)S(1)} %constant_dynamic-slice_fusion.1), channel_id=1, source_target_pairs={{0,4},{4,0},{1,5},{5,1},{2,6},{6,2},{3,7},{7,3},{8,12},{12,8},{9,1... | collective-permute-start | bytes 294920 | tf_op jit(solution)/shard_map/weight_swap/ppermute | solution.py:87
  79.6 2.4 %copy-start.16 = (bf16[8,1,128,128]{3,2,0,1:T(8,128)(2,1)}, bf16[8,1,128,128]{3,2,0,1:T(8,128)(2,1)S(1)}, u32[]{:S(2)}) copy-start(bf16[8,1,128,128]{3,2,0,1:T(8,128)(2,1)S(1)} %copy.53) | copy-start | bytes 786436
  82.7 23.2 %copy-start.17 = (bf16[8,1,128,768]{3,2,1,0:T(8,128)(2,1)S(1)}, bf16[8,1,128,768]{3,2,1,0:T(8,128)(2,1)}, u32[]{:S(2)}) copy-start(bf16[8,1,128,768]{3,2,1,0:T(8,128)(2,1)} %param.8) | copy-start | bytes 4718596
  82.7 22.9 %collective-permute-start.2 = (bf16[1024,128]{0,1:T(8,128)(2,1)S(1)}, bf16[1024,128]{0,1:T(8,128)(2,1)S(1)}, u32[]{:S(2)}, u32[]{:S(2)}) collective-permute-start(bf16[1024,128]{0,1:T(8,128)(2,1)S(1)} %convolution_convert_fusion.3), channel_id=1, source_target_pairs={{0,3},{1,0},{2,1},{3,2},{4,7},{5,4},{6,5},{7,6},{8,11},{9,8},{10,9... | collective-permute-start | bytes 786440 | tf_op jit(solution)/shard_map/head_gather/ppermute | solution.py:99
  85.2 20.3 %collective-permute-start.1 = (bf16[1024,128]{0,1:T(8,128)(2,1)S(1)}, bf16[1024,128]{0,1:T(8,128)(2,1)S(1)}, u32[]{:S(2)}, u32[]{:S(2)}) collective-permute-start(bf16[1024,128]{0,1:T(8,128)(2,1)S(1)} %convolution_convert_fusion.3), channel_id=1, source_target_pairs={{0,2},{1,3},{2,0},{3,1},{4,6},{5,7},{6,4},{7,5},{8,10},{9,11},{10,... | collective-permute-start | bytes 786440 | tf_op jit(solution)/shard_map/head_gather/ppermute | solution.py:99
  89.9 15.7 %collective-permute-start = (bf16[1024,128]{0,1:T(8,128)(2,1)S(1)}, bf16[1024,128]{0,1:T(8,128)(2,1)S(1)}, u32[]{:S(2)}, u32[]{:S(2)}) collective-permute-start(bf16[1024,128]{0,1:T(8,128)(2,1)S(1)} %convolution_convert_fusion.3), channel_id=1, source_target_pairs={{0,1},{1,2},{2,3},{3,0},{4,5},{5,6},{6,7},{7,4},{8,9},{9,10},{10,1... | collective-permute-start | bytes 786440 | tf_op jit(solution)/shard_map/head_gather/ppermute | solution.py:99
  123.5 2.6 %copy-start.19 = (bf16[8,1,128,768]{3,2,1,0:T(8,128)(2,1)S(1)}, bf16[8,1,128,768]{3,2,1,0:T(8,128)(2,1)}, u32[]{:S(2)}) copy-start(bf16[8,1,128,768]{3,2,1,0:T(8,128)(2,1)} %param.8) | copy-start | bytes 4718596
  123.5 2.8 %copy-start.20 = (bf16[1,2048,768]{2,1,0:T(8,128)(2,1)S(1)}, bf16[1,2048,768]{2,1,0:T(8,128)(2,1)}, u32[]{:S(2)}) copy-start(bf16[1,2048,768]{2,1,0:T(8,128)(2,1)} %all-gather.4.cloned.1.call-done) | copy-start | bytes 9437188
  126.4 6.8 %copy-start.5 = (bf16[1024,128]{0,1:T(8,128)(2,1)S(1)}, bf16[1024,128]{0,1:T(8,128)(2,1)}, u32[]{:S(2)}) copy-start(bf16[1024,128]{0,1:T(8,128)(2,1)} %copy-done.4) | copy-start | bytes 786436
  126.4 6.8 %copy-start.7 = (bf16[1024,128]{0,1:T(8,128)(2,1)S(1)}, bf16[1024,128]{0,1:T(8,128)(2,1)}, u32[]{:S(2)}) copy-start(bf16[1024,128]{0,1:T(8,128)(2,1)} %copy-done.6) | copy-start | bytes 786436
  126.4 6.8 %copy-start.9 = (bf16[1024,128]{0,1:T(8,128)(2,1)S(1)}, bf16[1024,128]{0,1:T(8,128)(2,1)}, u32[]{:S(2)}) copy-start(bf16[1024,128]{0,1:T(8,128)(2,1)} %copy-done.8) | copy-start | bytes 786436
  128.4 12.7 %all-to-all-start.1 = ((bf16[4,1024,128]{1,2,0:T(8,128)(2,1)}), bf16[4,1024,128]{1,2,0:T(8,128)(2,1)S(1)}, u32[]{:S(2)}, u32[]{:S(2)}) async-start(bf16[4,1024,128]{1,2,0:T(8,128)(2,1)} %bitcast.26), calls=%async_computation.2 | async-start | bytes 2097152 | tf_op jit(solution)/shard_map/head_grad/all_to_all | solution.py:118
  133.2 2.6 %copy-start.10 = (bf16[1024,128]{0,1:T(8,128)(2,1)S(1)}, bf16[1024,128]{0,1:T(8,128)(2,1)}, u32[]{:S(2)}) copy-start(bf16[1024,128]{0,1:T(8,128)(2,1)} %copy-done.8) | copy-start | bytes 786436
  133.2 2.6 %copy-start.21 = (bf16[1,2048,768]{2,1,0:T(8,128)(2,1)S(1)}, bf16[1,2048,768]{2,1,0:T(8,128)(2,1)}, u32[]{:S(2)}) copy-start(bf16[1,2048,768]{2,1,0:T(8,128)(2,1)} %all-gather.4.cloned.1.call-done) | copy-start | bytes 9437188
  136.9 19.1 %collective-permute-start.4 = (bf16[4,2,64,768]{3,2,0,1:T(8,128)(2,1)S(1)}, bf16[4,2,64,768]{3,2,0,1:T(8,128)(2,1)}, u32[]{:S(2)}, u32[]{:S(2)}) collective-permute-start(bf16[4,2,64,768]{3,2,0,1:T(8,128)(2,1)S(1)} %fusion.26), channel_id=1, source_target_pairs={{0,64},{64,0},{1,65},{65,1},{2,66},{66,2},{3,67},{67,3},{4,68},{68... | collective-permute-start | bytes 2359304 | tf_op jit(solution)/shard_map/weight_grad/ppermute | solution.py:54
  142.0 3.7 %copy-start.1 = (f32[1024,1024]{0,1:T(8,128)S(1)}, f32[1024,1024]{0,1:T(8,128)}, u32[]{:S(2)}) copy-start(f32[1024,1024]{0,1:T(8,128)} %copy-done) | copy-start | bytes 12582916
  150.0 58.1 %all-to-all-start.2 = ((bf16[8,3,128,128]{3,2,1,0:T(8,128)(2,1)}), bf16[8,3,128,128]{3,2,1,0:T(8,128)(2,1)S(1)}, u32[]{:S(2)}, u32[]{:S(2)}) async-start(bf16[8,3,128,128]{3,2,1,0:T(8,128)(2,1)} %pad_maximum_fusion.5), calls=%async_computation.3 | async-start | bytes 1572864 | tf_op jit(solution)/shard_map/qkv_return/all_to_all | solution.py:141
  157.4 10.6 %collective-permute-start.7 = (bf16[2,64,768]{2,1,0:T(8,128)(2,1)S(1)}, bf16[2,64,768]{2,1,0:T(8,128)(2,1)S(1)}, u32[]{:S(2)}, u32[]{:S(2)}) collective-permute-start(bf16[2,64,768]{2,1,0:T(8,128)(2,1)S(1)} %get-tuple-element.27), channel_id=1, source_target_pairs={{0,384},{128,0},{256,128},{384,256},{1,385},{129,1},{257,129},{385... | collective-permute-start | bytes 589832 | tf_op jit(solution)/shard_map/weight_grad/ppermute | solution.py:58
  159.8 10.1 %collective-permute-start.6 = (bf16[2,64,768]{2,1,0:T(8,128)(2,1)S(1)}, bf16[2,64,768]{2,1,0:T(8,128)(2,1)S(1)}, u32[]{:S(2)}, u32[]{:S(2)}) collective-permute-start(bf16[2,64,768]{2,1,0:T(8,128)(2,1)S(1)} %get-tuple-element.28), channel_id=1, source_target_pairs={{0,256},{128,384},{256,0},{384,128},{1,257},{129,385},{257,1},{385... | collective-permute-start | bytes 589832 | tf_op jit(solution)/shard_map/weight_grad/ppermute | solution.py:58
  164.3 8.3 %collective-permute-start.5 = (bf16[2,64,768]{2,1,0:T(8,128)(2,1)S(1)}, bf16[2,64,768]{2,1,0:T(8,128)(2,1)S(1)}, u32[]{:S(2)}, u32[]{:S(2)}) collective-permute-start(bf16[2,64,768]{2,1,0:T(8,128)(2,1)S(1)} %get-tuple-element.26), channel_id=1, source_target_pairs={{0,128},{128,256},{256,384},{384,0},{1,129},{129,257},{257,385},{3... | collective-permute-start | bytes 589832 | tf_op jit(solution)/shard_map/weight_grad/ppermute | solution.py:58
  172.7 20.5 %collective-permute-start.8 = (bf16[64,768]{1,0:T(8,128)(2,1)S(1)}, bf16[64,768]{1,0:T(8,128)(2,1)S(1)}, u32[]{:S(2)}, u32[]{:S(2)}) collective-permute-start(bf16[64,768]{1,0:T(8,128)(2,1)S(1)} %get-tuple-element.36), channel_id=1, source_target_pairs={{0,4},{4,0},{1,5},{5,1},{2,6},{6,2},{3,7},{7,3},{8,12},{12,8},{9,1... | collective-permute-start | bytes 294920 | tf_op jit(solution)/shard_map/weight_grad/ppermute | solution.py:129
  (12 other events, 16.5 us)
Sparse Core Ops, SparseCore 0:
  10.1 109.8 all-gather.3
  123.4 108.5 reduce-scatter.1

commit v3 on v2

--- a/solution.py
+++ b/solution.py
@@ -44,6 +44,26 @@
     return [[(i, (i + d) % count) for i in range(count)] for d in range(1, count)]
 
 
+def ring_pairs(step):
+    n_row, n_hi = lax.axis_size("row"), lax.axis_size("zhi")
+    spot = lambda z: (z % n_row) * n_hi + (z // n_row) % n_hi
+    return [(spot(z), spot(z + step)) for z in range(n_row * n_hi)]
+
+
+def ring_step(up, down):
+    return lax.ppermute(up, ("row", "zhi"), ring_pairs(1)), lax.ppermute(down, ("row", "zhi"), ring_pairs(-1))
+
+
+def ring_place(blocks):
+    count = lax.axis_size("row") * lax.axis_size("zhi")
+    rows, width = blocks[0].shape
+    z = lax.axis_index("zhi") * lax.axis_size("row") + lax.axis_index("row")
+    out = jnp.zeros((count * rows, width), blocks[0].dtype)
+    for d, block in blocks.items():
+        out = lax.dynamic_update_slice_in_dim(out, block, ((z + d) % count) * rows, 0)
+    return out
+
+
 def reduce_scatter_dp(blocks, piece):
     n_y, n_core = lax.axis_size("y"), lax.axis_size("core")
     y, core = lax.axis_index("y"), lax.axis_index("core")
@@ -70,13 +90,18 @@
     dp = lax.axis_index("y") * lax.axis_size("core") + lax.axis_index("core")
     swap = [(0, 1), (1, 0)]
 
-    with jax.named_scope("grad_gather"):
-        grad_all = lax.all_gather(out_grad[0], RING, axis=0, tiled=True).reshape(2, seq_len, width)
+    blocks = {0: out_grad[0]}
+    up = down = out_grad[0]
+    for d in range(1, 5):
+        with jax.named_scope("grad_gather"):
+            up, down = ring_step(up, down)
+            blocks[-d], blocks[d] = up, down
 
     with jax.named_scope("qkv_exchange"):
         by_head = lambda a: a[0].reshape(tok, n_row, HEAD_DIM).transpose(1, 0, 2)
         stacked = jnp.stack([by_head(queries), by_head(keys_in), by_head(values_in)], axis=1)
         heads = lax.all_to_all(stacked, ROW, 0, 0, tiled=True)
+        heads, up, down = lax.optimization_barrier((heads, up, down))
         query, key, value = (heads[:, i].reshape(seq_len, HEAD_DIM) for i in range(3))
 
     with jax.named_scope("weight_swap"):
@@ -94,9 +119,18 @@
     with jax.named_scope("attend"):
         head_out, probs = attention_forward(query, key, value)
 
+    with jax.named_scope("grad_gather"):
+        up, down = ring_step(up, down)
+        blocks[-5], blocks[5] = up, down
+        head_out, up, down = lax.optimization_barrier((head_out, up, down))
+        for d in (6, 7):
+            up, down = ring_step(up, down)
+            blocks[-d], blocks[d] = up, down
+
     with jax.named_scope("head_gather"):
         x_index = lax.axis_index("x")
         got = [head_out] + [lax.ppermute(head_out, "x", s) for s in shifts(n_x)]
+        *got, up, down = lax.optimization_barrier((*got, up, down))
         ordered = jnp.stack(got)
         heads_x = jnp.concatenate(
             [lax.dynamic_index_in_dim(ordered, (x_index - i) % n_x, 0, keepdims=False) for i in range(n_x)], axis=1
@@ -105,10 +139,15 @@
     with jax.named_scope("project"):
         part0 = jnp.dot(heads_x, w0, preferred_element_type=F32).astype(BF16)
         part1 = jnp.dot(heads_x, w1, preferred_element_type=F32).astype(BF16)
-        part0, part1, grad_all = lax.optimization_barrier((part0, part1, grad_all))
         parts = jnp.concatenate([part0, part1], axis=0)
+        projected = lax.psum_scatter(parts, RING, scatter_dimension=0, tiled=True)
+
+    with jax.named_scope("grad_gather"):
+        half = tok // 2
+        up, down = ring_step(up[:half], down[half:])
+        blocks[8] = jnp.concatenate([up, down], axis=0)
+        grad_all = ring_place(blocks).reshape(2, seq_len, width)
         parts, grad_all = lax.optimization_barrier((parts, grad_all))
-        projected = lax.psum_scatter(parts, RING, scatter_dimension=0, tiled=True)
 
     with jax.named_scope("head_grad"):
         over_n = (((1,), (1,)), ((), ()))

time: 240 us -> 294 us (1.23)
  the two profiles are of different devices: /device:TPU:12 before, /device:TPU:73 now
where the time goes in v3:
time: 294 us; the launch traced here: 293 us
  starting transfers between devices  114 us (39%)
  waiting for transfers between devices  64.5 us (22%)
  blocking collectives  48.1 us (16%)
  local copies, waits for them, and re-layouts  22.4 us (8%)
  matrix products  20.4 us (7%)
  between operations  14.7 us (5%)
  other arithmetic  9.05 us (3%)
    ppermute x1, waiting for transfers between devices, body(): arrived = lax.ppermute(away, 'zhi', swap)  32.5 us
    ppermute x8, starting transfers between devices, ring_step(): lax.ppermute(up, ('row', 'zhi'), ring_pairs(1))  32.4 us
    all_gather x1, blocking collectives, body(): own_rows = lax.all_gather(dw_own, DP, axis=0, tiled=True)  19.1 us
    ppermute x8, starting transfers between devices, ring_step(): lax.ppermute(down, ('row', 'zhi'), ring_pairs(-1))  15.8 us
    ppermute x1, waiting for transfers between devices, body(): dw_back = lax.ppermute(dw_away, 'zhi', swap)  15.5 us
    all_gather x1, blocking collectives, body(): other_rows = lax.all_gather(dw_back, DP, axis=0, tiled=True)  14.9 us
    all_gather x1, blocking collectives, body(): w_other = lax.all_gather(arrived, DP, axis=0, tiled=True)  14.1 us
    all_to_all x1, starting transfers between devices, body(): heads = lax.all_to_all(stacked, ROW, 0, 0, tiled=True)  11.6 us
  transfers between devices with their start and end apart: 29, of which 10 were waited for; matrix products, arithmetic and copies ran while one was open for 15% of the time, Pallas kernels for 0%

profile of v3, /device:TPU:73, one launch (start us, length us, event | category | flops | bytes accessed | tf_op | source)
XLA Modules:
  0.0 292.6 jit_solution(16165148430549248930)
XLA Ops:
  11.7 11.6 %all-to-all-start = ((bf16[8,3,128,128]{2,3,1,0:T(8,128)(2,1)}), bf16[8,3,128,128]{2,3,1,0:T(8,128)(2,1)S(1)}, u32[]{:S(2)}, u32[]{:S(2)}) async-start(bf16[8,3,128,128]{2,3,1,0:T(8,128)(2,1)} %copy.38), calls=%async_computation | async-start | bytes 1572864 | tf_op jit(solution)/shard_map/qkv_exchange/all_to_all | solution.py:103
  29.5 7.9 %collective-permute-start.17 = (bf16[64,768]{1,0:T(8,128)(2,1)S(1)}, bf16[64,768]{1,0:T(8,128)(2,1)S(1)}, u32[]{:S(2)}, u32[]{:S(2)}) collective-permute-start(bf16[64,768]{1,0:T(8,128)(2,1)S(1)} %constant_dynamic-slice_fusion.1), channel_id=1, source_target_pairs={{0,4},{4,0},{1,5},{5,1},{2,6},{6,2},{3,7},{7,3},{8,12},{12,8},{9,1... | collective-permute-start | bytes 294920 | tf_op jit(solution)/shard_map/weight_swap/ppermute | solution.py:112
  40.1 32.5 %collective-permute-done.17 = bf16[64,768]{1,0:T(8,128)(2,1)S(1)} collective-permute-done((bf16[64,768]{1,0:T(8,128)(2,1)S(1)}, bf16[64,768]{1,0:T(8,128)(2,1)S(1)}, u32[]{:S(2)}, u32[]{:S(2)}) %collective-permute-start.17) | collective-permute-done | bytes 98336 | tf_op jit(solution)/shard_map/weight_swap/ppermute | solution.py:112
  72.6 14.1 %all_gather.9 = bf16[512,768]{1,0:T(8,128)(2,1)S(1)} all-gather(bf16[64,768]{1,0:T(8,128)(2,1)S(1)} %collective-permute-done.17), channel_id=1, replica_groups=mesh['y'=4,'core'=2,'row'=8,'zhi'=2,'x'=4] {'y','core'}, dimensions={0}, use_global_device_ids=true | all-gather | bytes 884736 | tf_op jit(solution)/shard_map/weight_swap/all_gather | solution.py:113
  88.6 3.4 %collective-permute-start.1 = (bf16[128,768]{1,0:T(8,128)(2,1)S(1)}, bf16[128,768]{1,0:T(8,128)(2,1)S(1)}, u32[]{:S(2)}, u32[]{:S(2)}) collective-permute-start(bf16[128,768]{1,0:T(8,128)(2,1)S(1)} %collective-permute-done), channel_id=1, source_target_pairs={{0,8},{8,16},{16,24},{24,32},{32,40},{40,48},{48,56},{56,4},{4,12}... | collective-permute-start | bytes 589832 | tf_op jit(solution)/shard_map/grad_gather/ppermute | solution.py:54
  97.1 6.0 %collective-permute-start.2 = (bf16[128,768]{1,0:T(8,128)(2,1)S(1)}, bf16[128,768]{1,0:T(8,128)(2,1)S(1)}, u32[]{:S(2)}, u32[]{:S(2)}) collective-permute-start(bf16[128,768]{1,0:T(8,128)(2,1)S(1)} %collective-permute-done.1), channel_id=1, source_target_pairs={{0,8},{8,16},{16,24},{24,32},{32,40},{40,48},{48,56},{56,4},{4,12}... | collective-permute-start | bytes 589832 | tf_op jit(solution)/shard_map/grad_gather/ppermute | solution.py:54
  107.6 4.3 %collective-permute-start.3 = (bf16[128,768]{1,0:T(8,128)(2,1)S(1)}, bf16[128,768]{1,0:T(8,128)(2,1)S(1)}, u32[]{:S(2)}, u32[]{:S(2)}) collective-permute-start(bf16[128,768]{1,0:T(8,128)(2,1)S(1)} %collective-permute-done.2), channel_id=1, source_target_pairs={{0,8},{8,16},{16,24},{24,32},{32,40},{40,48},{48,56},{56,4},{4,12}... | collective-permute-start | bytes 589832 | tf_op jit(solution)/shard_map/grad_gather/ppermute | solution.py:54
  116.4 4.4 %collective-permute-start.8 = (bf16[128,768]{1,0:T(8,128)(2,1)S(1)}, bf16[128,768]{1,0:T(8,128)(2,1)S(1)}, u32[]{:S(2)}, u32[]{:S(2)}) collective-permute-start(bf16[128,768]{1,0:T(8,128)(2,1)S(1)} %collective-permute-done.3), channel_id=1, source_target_pairs={{0,8},{8,16},{16,24},{24,32},{32,40},{40,48},{48,56},{56,4},{4,12}... | collective-permute-start | bytes 589832 | tf_op jit(solution)/shard_map/grad_gather/ppermute | solution.py:54
  125.5 3.4 %collective-permute-done.9 = bf16[128,768]{1,0:T(8,128)(2,1)S(1)} collective-permute-done((bf16[128,768]{1,0:T(8,128)(2,1)S(1)}, bf16[128,768]{1,0:T(8,128)(2,1)S(1)}, u32[]{:S(2)}, u32[]{:S(2)}) %collective-permute-start.9) | collective-permute-done | bytes 196640 | tf_op jit(solution)/shard_map/grad_gather/ppermute | solution.py:54
  129.0 4.4 %collective-permute-start.12 = (bf16[1024,128]{1,0:T(8,128)(2,1)S(1)}, bf16[1024,128]{1,0:T(8,128)(2,1)S(1)}, u32[]{:S(2)}, u32[]{:S(2)}) collective-permute-start(bf16[1024,128]{1,0:T(8,128)(2,1)S(1)} %convolution_convert_fusion.3), channel_id=1, source_target_pairs={{0,3},{1,0},{2,1},{3,2},{4,7},{5,4},{6,5},{7,6},{8,11},{9,8},{10,9... | collective-permute-start | bytes 786440 | tf_op jit(solution)/shard_map/head_gather/ppermute | solution.py:132
  138.3 4.6 %collective-permute-start.13 = (bf16[128,768]{1,0:T(8,128)(2,1)S(1)}, bf16[128,768]{1,0:T(8,128)(2,1)S(1)}, u32[]{:S(2)}, u32[]{:S(2)}) collective-permute-start(bf16[128,768]{1,0:T(8,128)(2,1)S(1)} %collective-permute-done.8), channel_id=1, source_target_pairs={{0,8},{8,16},{16,24},{24,32},{32,40},{40,48},{48,56},{56,4},{4,12}... | collective-permute-start | bytes 589832 | tf_op jit(solution)/shard_map/grad_gather/ppermute | solution.py:54
  146.2 3.4 %collective-permute-start.14 = (bf16[128,768]{1,0:T(8,128)(2,1)S(1)}, bf16[128,768]{1,0:T(8,128)(2,1)S(1)}, u32[]{:S(2)}, u32[]{:S(2)}) collective-permute-start(bf16[128,768]{1,0:T(8,128)(2,1)S(1)} %collective-permute-done.13), channel_id=1, source_target_pairs={{0,8},{8,16},{16,24},{24,32},{32,40},{40,48},{48,56},{56,4},{4,12}... | collective-permute-start | bytes 589832 | tf_op jit(solution)/shard_map/grad_gather/ppermute | solution.py:54
  153.4 4.1 %collective-permute-done.16 = bf16[128,768]{1,0:T(8,128)(2,1)S(1)} collective-permute-done((bf16[128,768]{1,0:T(8,128)(2,1)S(1)}, bf16[128,768]{1,0:T(8,128)(2,1)S(1)}, u32[]{:S(2)}, u32[]{:S(2)}) %collective-permute-start.16) | collective-permute-done | bytes 196640 | tf_op jit(solution)/shard_map/grad_gather/ppermute | solution.py:54
  171.8 3.4 %add_convert_fusion = bf16[1024,512]{0,1:T(8,128)(2,1)} fusion(f32[1024,512]{0,1:T(8,128)S(1)} %fusion.6, bf16[2,1024,768]{2,1,0:T(8,128)(2,1)} %bitcast.23, bf16[512,768]{1,0:T(8,128)(2,1)S(1)} %all_gather.9, pred[]{:T(512)S(6)} %eq.27, bf16[1024,768]{1,0:T(8,128)(2,1)S(1)} %bitcast.140, s32[]{:T(128)S(6)} %select_n.223), kind=kOutput, calls=%fused_computation.9 | convolution fusion | flops 806748160 | bytes 6291461 | tf_op jit(solution)/shard_map/head_grad/dot_general | solution.py:154
  175.2 3.7 %all-to-all-start.1 = ((bf16[4,1024,128]{1,2,0:T(8,128)(2,1)}), bf16[4,1024,128]{1,2,0:T(8,128)(2,1)S(1)}, u32[]{:S(2)}, u32[]{:S(2)}) async-start(bf16[4,1024,128]{1,2,0:T(8,128)(2,1)} %bitcast.27), calls=%async_computation.2 | async-start | bytes 2097152 | tf_op jit(solution)/shard_map/head_grad/all_to_all | solution.py:157
  184.0 10.4 %collective-permute-start.20 = (bf16[4,2,64,768]{3,2,0,1:T(8,128)(2,1)S(1)}, bf16[4,2,64,768]{3,2,0,1:T(8,128)(2,1)}, u32[]{:S(2)}, u32[]{:S(2)}) collective-permute-start(bf16[4,2,64,768]{3,2,0,1:T(8,128)(2,1)S(1)} %fusion.26), channel_id=1, source_target_pairs={{0,64},{64,0},{1,65},{65,1},{2,66},{66,2},{3,67},{67,3},{4,68},{68... | collective-permute-start | bytes 2359304 | tf_op jit(solution)/shard_map/weight_grad/ppermute | solution.py:74
  195.4 3.4 %multiply_reduce_fusion = (f32[1024]{0:T(1024)S(1)}, f32[1024,1024]{0,1:T(8,128)S(1)}) fusion(f32[1024]{0:T(1024)S(1)} %fusion.1, f32[1024]{0:T(1024)S(1)} %get-tuple-element.53, f32[1024,1024]{0,1:T(8,128)} %copy-done, bf16[1024,128]{1,0:T(8,128)(2,1)} %bitcast.126, bf16[1024,128]{0,1:T(8,128)(2,1)} %reduce_sum.31), kind=kOutput, calls=%fused_computation.1 | convolution fusion | flops 275774464 | bytes 8925184 | tf_op jit(solution)/shard_map/attend_back/dot_general | solution.py:33
  203.3 6.9 %all-to-all-start.2 = ((bf16[8,3,128,128]{3,2,1,0:T(8,128)(2,1)}), bf16[8,3,128,128]{3,2,1,0:T(8,128)(2,1)S(1)}, u32[]{:S(2)}, u32[]{:S(2)}) async-start(bf16[8,3,128,128]{3,2,1,0:T(8,128)(2,1)} %pad_maximum_fusion.5), calls=%async_computation.3 | async-start | bytes 1572864 | tf_op jit(solution)/shard_map/qkv_return/all_to_all | solution.py:180
  216.9 3.7 %collective-permute-start.22 = (bf16[2,64,768]{2,1,0:T(8,128)(2,1)S(1)}, bf16[2,64,768]{2,1,0:T(8,128)(2,1)S(1)}, u32[]{:S(2)}, u32[]{:S(2)}) collective-permute-start(bf16[2,64,768]{2,1,0:T(8,128)(2,1)S(1)} %get-tuple-element.44), channel_id=1, source_target_pairs={{0,256},{128,384},{256,0},{384,128},{1,257},{129,385},{257,1},{385... | collective-permute-start | bytes 589832 | tf_op jit(solution)/shard_map/weight_grad/ppermute | solution.py:78
  221.0 4.0 %collective-permute-done.22 = bf16[2,64,768]{2,1,0:T(8,128)(2,1)S(1)} collective-permute-done((bf16[2,64,768]{2,1,0:T(8,128)(2,1)S(1)}, bf16[2,64,768]{2,1,0:T(8,128)(2,1)S(1)}, u32[]{:S(2)}, u32[]{:S(2)}) %collective-permute-start.22) | collective-permute-done | bytes 196640 | tf_op jit(solution)/shard_map/weight_grad/ppermute | solution.py:78
  225.1 6.4 %collective-permute-start.24 = (bf16[64,768]{1,0:T(8,128)(2,1)S(1)}, bf16[64,768]{1,0:T(8,128)(2,1)S(1)}, u32[]{:S(2)}, u32[]{:S(2)}) collective-permute-start(bf16[64,768]{1,0:T(8,128)(2,1)S(1)} %get-tuple-element.52), channel_id=1, source_target_pairs={{0,4},{4,0},{1,5},{5,1},{2,6},{6,2},{3,7},{7,3},{8,12},{12,8},{9,1... | collective-permute-start | bytes 294920 | tf_op jit(solution)/shard_map/weight_grad/ppermute | solution.py:168
  231.6 19.1 %all-gather = bf16[1,512,768]{2,1,0:T(8,128)(2,1)S(1)} all-gather(bf16[1,64,768]{2,1,0:T(8,128)(2,1)S(1)} %get-tuple-element.51), channel_id=2, replica_groups=mesh['y'=4,'core'=2,'row'=8,'zhi'=2,'x'=4] {'y','core'}, dimensions={1}, use_global_device_ids=true | all-gather | bytes 884736 | tf_op jit(solution)/shard_map/weight_grad/all_gather | solution.py:169
  250.7 15.5 %collective-permute-done.24 = bf16[64,768]{1,0:T(8,128)(2,1)S(1)} collective-permute-done((bf16[64,768]{1,0:T(8,128)(2,1)S(1)}, bf16[64,768]{1,0:T(8,128)(2,1)S(1)}, u32[]{:S(2)}, u32[]{:S(2)}) %collective-permute-start.24) | collective-permute-done | bytes 98336 | tf_op jit(solution)/shard_map/weight_grad/ppermute | solution.py:168
  266.2 14.9 %all_gather.11 = bf16[512,768]{1,0:T(8,128)(2,1)S(1)} all-gather(bf16[64,768]{1,0:T(8,128)(2,1)S(1)} %collective-permute-done.24), channel_id=1, replica_groups=mesh['y'=4,'core'=2,'row'=8,'zhi'=2,'x'=4] {'y','core'}, dimensions={0}, use_global_device_ids=true | all-gather | bytes 884736 | tf_op jit(solution)/shard_map/weight_grad/all_gather | solution.py:170
  (122 shorter events, 82.4 us)
Async XLA Ops:
  11.7 104.3 %all-to-all-start = ((bf16[8,3,128,128]{2,3,1,0:T(8,128)(2,1)}), bf16[8,3,128,128]{2,3,1,0:T(8,128)(2,1)S(1)}, u32[]{:S(2)}, u32[]{:S(2)}) async-start(bf16[8,3,128,128]{2,3,1,0:T(8,128)(2,1)} %copy.38), calls=%async_computation | async-start | bytes 1572864 | tf_op jit(solution)/shard_map/qkv_exchange/all_to_all | solution.py:103
  23.3 262.5 %reduce-scatter.2.cloned.1.call-start = ((), (), s32[]{:S(2)}) async-start(), calls=%async_computation.4 | async-start | bytes 3342336 | tf_op jit(solution)/shard_map/project/reduce_scatter | solution.py:143
  23.3 63.4 %collective-permute-start.4 = (bf16[128,768]{1,0:T(8,128)(2,1)S(1)}, bf16[128,768]{1,0:T(8,128)(2,1)S(1)}, u32[]{:S(2)}, u32[]{:S(2)}) collective-permute-start(bf16[128,768]{1,0:T(8,128)(2,1)S(1)} %bitcast.134), channel_id=1, source_target_pairs={{0,60},{8,0},{16,8},{24,16},{32,24},{40,32},{48,40},{56,48},{4,56}... | collective-permute-start | bytes 589832 | tf_op jit(solution)/shard_map/grad_gather/ppermute | solution.py:54
  25.5 63.1 %collective-permute-start = (bf16[128,768]{1,0:T(8,128)(2,1)S(1)}, bf16[128,768]{1,0:T(8,128)(2,1)S(1)}, u32[]{:S(2)}, u32[]{:S(2)}) collective-permute-start(bf16[128,768]{1,0:T(8,128)(2,1)S(1)} %bitcast.135), channel_id=1, source_target_pairs={{0,8},{8,16},{16,24},{24,32},{32,40},{40,48},{48,56},{56,4},{4,12}... | collective-permute-start | bytes 589832 | tf_op jit(solution)/shard_map/grad_gather/ppermute | solution.py:54
  29.5 43.1 %collective-permute-start.17 = (bf16[64,768]{1,0:T(8,128)(2,1)S(1)}, bf16[64,768]{1,0:T(8,128)(2,1)S(1)}, u32[]{:S(2)}, u32[]{:S(2)}) collective-permute-start(bf16[64,768]{1,0:T(8,128)(2,1)S(1)} %constant_dynamic-slice_fusion.1), channel_id=1, source_target_pairs={{0,4},{4,0},{1,5},{5,1},{2,6},{6,2},{3,7},{7,3},{8,12},{12,8},{9,1... | collective-permute-start | bytes 294920 | tf_op jit(solution)/shard_map/weight_swap/ppermute | solution.py:112
  86.7 8.2 %collective-permute-start.5 = (bf16[128,768]{1,0:T(8,128)(2,1)S(1)}, bf16[128,768]{1,0:T(8,128)(2,1)S(1)}, u32[]{:S(2)}, u32[]{:S(2)}) collective-permute-start(bf16[128,768]{1,0:T(8,128)(2,1)S(1)} %collective-permute-done.4), channel_id=1, source_target_pairs={{0,60},{8,0},{16,8},{24,16},{32,24},{40,32},{48,40},{56,48},{4,56}... | collective-permute-start | bytes 589832 | tf_op jit(solution)/shard_map/grad_gather/ppermute | solution.py:54
  88.6 8.5 %collective-permute-start.1 = (bf16[128,768]{1,0:T(8,128)(2,1)S(1)}, bf16[128,768]{1,0:T(8,128)(2,1)S(1)}, u32[]{:S(2)}, u32[]{:S(2)}) collective-permute-start(bf16[128,768]{1,0:T(8,128)(2,1)S(1)} %collective-permute-done), channel_id=1, source_target_pairs={{0,8},{8,16},{16,24},{24,32},{32,40},{40,48},{48,56},{56,4},{4,12}... | collective-permute-start | bytes 589832 | tf_op jit(solution)/shard_map/grad_gather/ppermute | solution.py:54
  94.9 10.7 %collective-permute-start.6 = (bf16[128,768]{1,0:T(8,128)(2,1)S(1)}, bf16[128,768]{1,0:T(8,128)(2,1)S(1)}, u32[]{:S(2)}, u32[]{:S(2)}) collective-permute-start(bf16[128,768]{1,0:T(8,128)(2,1)S(1)} %collective-permute-done.5), channel_id=1, source_target_pairs={{0,60},{8,0},{16,8},{24,16},{32,24},{40,32},{48,40},{56,48},{4,56}... | collective-permute-start | bytes 589832 | tf_op jit(solution)/shard_map/grad_gather/ppermute | solution.py:54
  97.1 10.5 %collective-permute-start.2 = (bf16[128,768]{1,0:T(8,128)(2,1)S(1)}, bf16[128,768]{1,0:T(8,128)(2,1)S(1)}, u32[]{:S(2)}, u32[]{:S(2)}) collective-permute-start(bf16[128,768]{1,0:T(8,128)(2,1)S(1)} %collective-permute-done.1), channel_id=1, source_target_pairs={{0,8},{8,16},{16,24},{24,32},{32,40},{40,48},{48,56},{56,4},{4,12}... | collective-permute-start | bytes 589832 | tf_op jit(solution)/shard_map/grad_gather/ppermute | solution.py:54
  105.6 9.6 %collective-permute-start.7 = (bf16[128,768]{1,0:T(8,128)(2,1)S(1)}, bf16[128,768]{1,0:T(8,128)(2,1)S(1)}, u32[]{:S(2)}, u32[]{:S(2)}) collective-permute-start(bf16[128,768]{1,0:T(8,128)(2,1)S(1)} %collective-permute-done.6), channel_id=1, source_target_pairs={{0,60},{8,0},{16,8},{24,16},{32,24},{40,32},{48,40},{56,48},{4,56}... | collective-permute-start | bytes 589832 | tf_op jit(solution)/shard_map/grad_gather/ppermute | solution.py:54
  116.4 9.1 %collective-permute-start.8 = (bf16[128,768]{1,0:T(8,128)(2,1)S(1)}, bf16[128,768]{1,0:T(8,128)(2,1)S(1)}, u32[]{:S(2)}, u32[]{:S(2)}) collective-permute-start(bf16[128,768]{1,0:T(8,128)(2,1)S(1)} %collective-permute-done.3), channel_id=1, source_target_pairs={{0,8},{8,16},{16,24},{24,32},{32,40},{40,48},{48,56},{56,4},{4,12}... | collective-permute-start | bytes 589832 | tf_op jit(solution)/shard_map/grad_gather/ppermute | solution.py:54
  120.9 8.1 %collective-permute-start.9 = (bf16[128,768]{1,0:T(8,128)(2,1)S(1)}, bf16[128,768]{1,0:T(8,128)(2,1)S(1)}, u32[]{:S(2)}, u32[]{:S(2)}) collective-permute-start(bf16[128,768]{1,0:T(8,128)(2,1)S(1)} %collective-permute-done.7), channel_id=1, source_target_pairs={{0,60},{8,0},{16,8},{24,16},{32,24},{40,32},{48,40},{56,48},{4,56}... | collective-permute-start | bytes 589832 | tf_op jit(solution)/shard_map/grad_gather/ppermute | solution.py:54
  129.0 23.9 %collective-permute-start.12 = (bf16[1024,128]{1,0:T(8,128)(2,1)S(1)}, bf16[1024,128]{1,0:T(8,128)(2,1)S(1)}, u32[]{:S(2)}, u32[]{:S(2)}) collective-permute-start(bf16[1024,128]{1,0:T(8,128)(2,1)S(1)} %convolution_convert_fusion.3), channel_id=1, source_target_pairs={{0,3},{1,0},{2,1},{3,2},{4,7},{5,4},{6,5},{7,6},{8,11},{9,8},{10,9... | collective-permute-start | bytes 786440 | tf_op jit(solution)/shard_map/head_gather/ppermute | solution.py:132
  133.3 19.5 %collective-permute-start.11 = (bf16[1024,128]{1,0:T(8,128)(2,1)S(1)}, bf16[1024,128]{1,0:T(8,128)(2,1)S(1)}, u32[]{:S(2)}, u32[]{:S(2)}) collective-permute-start(bf16[1024,128]{1,0:T(8,128)(2,1)S(1)} %convolution_convert_fusion.3), channel_id=1, source_target_pairs={{0,2},{1,3},{2,0},{3,1},{4,6},{5,7},{6,4},{7,5},{8,10},{9,11},{10,... | collective-permute-start | bytes 786440 | tf_op jit(solution)/shard_map/head_gather/ppermute | solution.py:132
  135.8 17.1 %collective-permute-start.10 = (bf16[1024,128]{1,0:T(8,128)(2,1)S(1)}, bf16[1024,128]{1,0:T(8,128)(2,1)S(1)}, u32[]{:S(2)}, u32[]{:S(2)}) collective-permute-start(bf16[1024,128]{1,0:T(8,128)(2,1)S(1)} %convolution_convert_fusion.3), channel_id=1, source_target_pairs={{0,1},{1,2},{2,3},{3,0},{4,5},{5,6},{6,7},{7,4},{8,9},{9,10},{10,1... | collective-permute-start | bytes 786440 | tf_op jit(solution)/shard_map/head_gather/ppermute | solution.py:132
  138.3 7.9 %collective-permute-start.13 = (bf16[128,768]{1,0:T(8,128)(2,1)S(1)}, bf16[128,768]{1,0:T(8,128)(2,1)S(1)}, u32[]{:S(2)}, u32[]{:S(2)}) collective-permute-start(bf16[128,768]{1,0:T(8,128)(2,1)S(1)} %collective-permute-done.8), channel_id=1, source_target_pairs={{0,8},{8,16},{16,24},{24,32},{32,40},{40,48},{48,56},{56,4},{4,12}... | collective-permute-start | bytes 589832 | tf_op jit(solution)/shard_map/grad_gather/ppermute | solution.py:54
  149.6 7.9 %collective-permute-start.16 = (bf16[128,768]{1,0:T(8,128)(2,1)S(1)}, bf16[128,768]{1,0:T(8,128)(2,1)S(1)}, u32[]{:S(2)}, u32[]{:S(2)}) collective-permute-start(bf16[128,768]{1,0:T(8,128)(2,1)S(1)} %collective-permute-done.15), channel_id=1, source_target_pairs={{0,60},{8,0},{16,8},{24,16},{32,24},{40,32},{48,40},{56,48},{4,56}... | collective-permute-start | bytes 589832 | tf_op jit(solution)/shard_map/grad_gather/ppermute | solution.py:54
  159.8 8.6 %collective-permute-start.19 = (bf16[64,768]{1,0:T(8,128)(2,1)S(1)}, bf16[64,768]{1,0:T(8,128)(2,1)S(1)}, u32[]{:S(2)}, u32[]{:S(2)}) collective-permute-start(bf16[64,768]{1,0:T(8,128)(2,1)S(1)} %slice.36), channel_id=1, source_target_pairs={{0,60},{8,0},{16,8},{24,16},{32,24},{40,32},{48,40},{56,48},{4,56}... | collective-permute-start | bytes 294920 | tf_op jit(solution)/shard_map/grad_gather/ppermute | solution.py:54
  175.2 19.2 %all-to-all-start.1 = ((bf16[4,1024,128]{1,2,0:T(8,128)(2,1)}), bf16[4,1024,128]{1,2,0:T(8,128)(2,1)S(1)}, u32[]{:S(2)}, u32[]{:S(2)}) async-start(bf16[4,1024,128]{1,2,0:T(8,128)(2,1)} %bitcast.27), calls=%async_computation.2 | async-start | bytes 2097152 | tf_op jit(solution)/shard_map/head_grad/all_to_all | solution.py:157
  184.0 26.2 %collective-permute-start.20 = (bf16[4,2,64,768]{3,2,0,1:T(8,128)(2,1)S(1)}, bf16[4,2,64,768]{3,2,0,1:T(8,128)(2,1)}, u32[]{:S(2)}, u32[]{:S(2)}) collective-permute-start(bf16[4,2,64,768]{3,2,0,1:T(8,128)(2,1)S(1)} %fusion.26), channel_id=1, source_target_pairs={{0,64},{64,0},{1,65},{65,1},{2,66},{66,2},{3,67},{67,3},{4,68},{68... | collective-permute-start | bytes 2359304 | tf_op jit(solution)/shard_map/weight_grad/ppermute | solution.py:74
  203.3 79.2 %all-to-all-start.2 = ((bf16[8,3,128,128]{3,2,1,0:T(8,128)(2,1)}), bf16[8,3,128,128]{3,2,1,0:T(8,128)(2,1)S(1)}, u32[]{:S(2)}, u32[]{:S(2)}) async-start(bf16[8,3,128,128]{3,2,1,0:T(8,128)(2,1)} %pad_maximum_fusion.5), calls=%async_computation.3 | async-start | bytes 1572864 | tf_op jit(solution)/shard_map/qkv_return/all_to_all | solution.py:180
  211.6 9.0 %collective-permute-start.21 = (bf16[2,64,768]{2,1,0:T(8,128)(2,1)S(1)}, bf16[2,64,768]{2,1,0:T(8,128)(2,1)S(1)}, u32[]{:S(2)}, u32[]{:S(2)}) collective-permute-start(bf16[2,64,768]{2,1,0:T(8,128)(2,1)S(1)} %get-tuple-element.42), channel_id=1, source_target_pairs={{0,128},{128,256},{256,384},{384,0},{1,129},{129,257},{257,385},{3... | collective-permute-start | bytes 589832 | tf_op jit(solution)/shard_map/weight_grad/ppermute | solution.py:78
  216.9 8.1 %collective-permute-start.22 = (bf16[2,64,768]{2,1,0:T(8,128)(2,1)S(1)}, bf16[2,64,768]{2,1,0:T(8,128)(2,1)S(1)}, u32[]{:S(2)}, u32[]{:S(2)}) collective-permute-start(bf16[2,64,768]{2,1,0:T(8,128)(2,1)S(1)} %get-tuple-element.44), channel_id=1, source_target_pairs={{0,256},{128,384},{256,0},{384,128},{1,257},{129,385},{257,1},{385... | collective-permute-start | bytes 589832 | tf_op jit(solution)/shard_map/weight_grad/ppermute | solution.py:78
  225.1 41.1 %collective-permute-start.24 = (bf16[64,768]{1,0:T(8,128)(2,1)S(1)}, bf16[64,768]{1,0:T(8,128)(2,1)S(1)}, u32[]{:S(2)}, u32[]{:S(2)}) collective-permute-start(bf16[64,768]{1,0:T(8,128)(2,1)S(1)} %get-tuple-element.52), channel_id=1, source_target_pairs={{0,4},{4,0},{1,5},{5,1},{2,6},{6,2},{3,7},{7,3},{8,12},{12,8},{9,1... | collective-permute-start | bytes 294920 | tf_op jit(solution)/shard_map/weight_grad/ppermute | solution.py:168
  (17 other events, 139.1 us)
Sparse Core Ops, SparseCore 0:
  167.1 106.4 reduce-scatter.1

commit v4 on v2

--- a/solution.py
+++ b/solution.py
@@ -1,8 +1,11 @@
+import functools
 import math
 
 import jax
 import jax.numpy as jnp
 from jax import lax
+from jax.experimental import pallas as pl
+from jax.experimental.pallas import tpu as pltpu
 from jax.sharding import Mesh, PartitionSpec as P
 
 HEAD_DIM = 128
@@ -25,23 +28,89 @@
     expo = jnp.exp(scores - row_max)
     probs = expo / jnp.sum(expo, axis=-1, keepdims=True)
     head_out = jnp.dot(probs.astype(BF16), value, preferred_element_type=F32).astype(BF16)
-    return head_out, probs
-
-
-def attention_backward(query, key, value, probs, grad):
+    return head_out
+
+
+def backward_kernel(span, n_x, tok, query_ref, key_ref, value_ref, parts_ref, out_ref, key_sum, value_sum):
+    seq_len = query_ref.shape[0]
     scale = 1.0 / math.sqrt(HEAD_DIM)
-    dprobs = lax.dot_general(grad, value, (((1,), (1,)), ((), ())), preferred_element_type=F32)
-    row_dot = jnp.sum(probs * dprobs, axis=-1, keepdims=True)
-    dscores = (probs * (dprobs - row_dot)).astype(BF16)
-    d_query = (jnp.dot(dscores, key, preferred_element_type=F32) * scale).astype(BF16)
+    over_cols = (((1,), (1,)), ((), ()))
     over_rows = (((0,), (0,)), ((), ()))
-    d_key = (lax.dot_general(dscores, query, over_rows, preferred_element_type=F32) * scale).astype(BF16)
-    d_value = lax.dot_general(probs.astype(BF16), grad, over_rows, preferred_element_type=F32).astype(BF16)
-    return d_query, d_key, d_value
+    key_sum[...] = jnp.zeros_like(key_sum)
+    value_sum[...] = jnp.zeros_like(value_sum)
+    for first in range(0, seq_len, span):
+        past = first + span
+        query = query_ref[first:past, :]
+        key = key_ref[:past, :]
+        value = value_ref[:past, :]
+        grad = parts_ref[0, first:past, :].astype(F32)
+        for i in range(1, n_x):
+            grad = grad + parts_ref[i, first:past, :].astype(F32)
+        grad = grad.astype(BF16)
+        scores = lax.dot_general(query, key, over_cols, preferred_element_type=F32) * scale
+        row = lax.broadcasted_iota(jnp.int32, scores.shape, 0) + first
+        col = lax.broadcasted_iota(jnp.int32, scores.shape, 1)
+        scores = jnp.where(col <= row, scores, F32(-1e30))
+        expo = jnp.exp(scores - jnp.max(scores, axis=-1, keepdims=True))
+        probs = expo * (1.0 / jnp.sum(expo, axis=-1, keepdims=True))
+        dprobs = lax.dot_general(grad, value, over_cols, preferred_element_type=F32)
+        row_dot = jnp.sum(probs * dprobs, axis=-1, keepdims=True)
+        dscores = (probs * (dprobs - row_dot)).astype(BF16)
+        d_query = (jnp.dot(dscores, key, preferred_element_type=F32) * scale).astype(BF16)
+        out_ref[first // tok : past // tok, 0] = d_query.reshape(span // tok, tok, HEAD_DIM)
+        key_sum[:past, :] += lax.dot_general(dscores, query, over_rows, preferred_element_type=F32)
+        value_sum[:past, :] += lax.dot_general(probs.astype(BF16), grad, over_rows, preferred_element_type=F32)
+    blocks = (seq_len // tok, tok, HEAD_DIM)
+    out_ref[:, 1] = (key_sum[...] * scale).astype(BF16).reshape(blocks)
+    out_ref[:, 2] = value_sum[...].astype(BF16).reshape(blocks)
+
+
+def attention_backward(query, key, value, parts, tok):
+    seq_len = query.shape[0]
+    n_x = parts.shape[0]
+    span = min(seq_len, 256)
+    vmem = pl.BlockSpec(memory_space=pltpu.VMEM)
+    return pl.pallas_call(
+        functools.partial(backward_kernel, span, n_x, tok),
+        out_shape=jax.ShapeDtypeStruct((seq_len // tok, 3, tok, HEAD_DIM), BF16),
+        in_specs=[vmem] * 4,
+        out_specs=vmem,
+        scratch_shapes=[pltpu.VMEM((seq_len, HEAD_DIM), F32)] * 2,
+        compiler_params=pltpu.CompilerParams(vmem_limit_bytes=40 * 1024 * 1024),
+        cost_estimate=pl.CostEstimate(
+            flops=14 * seq_len * seq_len * HEAD_DIM // 2, bytes_accessed=16 * seq_len * HEAD_DIM, transcendentals=seq_len * seq_len // 2
+        ),
+    )(query, key, value, parts)
 
 
 def shifts(count):
     return [[(i, (i + d) % count) for i in range(count)] for d in range(1, count)]
+
+
+def spread_heads(arrays):
+    n_row, row = lax.axis_size("row"), lax.axis_index("row")
+    tok = arrays[0].shape[0]
+    cut = lambda j: jnp.stack([lax.dynamic_slice_in_dim(a, j * HEAD_DIM, HEAD_DIM, 1) for a in arrays])
+    out = jnp.zeros((len(arrays), n_row * tok, HEAD_DIM), arrays[0].dtype)
+    put = lambda out, part, t: lax.dynamic_update_slice_in_dim(out, part, t * tok, 1)
+    got = [lax.ppermute(cut((row + d) % n_row), "row", pairs) for d, pairs in enumerate(shifts(n_row), 1)]
+    out = put(out, cut(row), row)
+    for d, part in enumerate(got, 1):
+        out = put(out, part, (row - d) % n_row)
+    return [out[i] for i in range(len(arrays))]
+
+
+def return_heads(arrays):
+    n_row, row = lax.axis_size("row"), lax.axis_index("row")
+    tok = arrays[0].shape[0] // n_row
+    cut = lambda t: jnp.stack([lax.dynamic_slice_in_dim(a, t * tok, tok, 0) for a in arrays])
+    out = jnp.zeros((len(arrays), tok, n_row * HEAD_DIM), arrays[0].dtype)
+    put = lambda out, part, j: lax.dynamic_update_slice_in_dim(out, part, j * HEAD_DIM, 2)
+    got = [lax.ppermute(cut((row + d) % n_row), "row", pairs) for d, pairs in enumerate(shifts(n_row), 1)]
+    out = put(out, cut(row), row)
+    for d, part in enumerate(got, 1):
+        out = put(out, part, (row - d) % n_row)
+    return [out[i] for i in range(len(arrays))]
 
 
 def reduce_scatter_dp(blocks, piece):
@@ -74,10 +143,7 @@
         grad_all = lax.all_gather(out_grad[0], RING, axis=0, tiled=True).reshape(2, seq_len, width)
 
     with jax.named_scope("qkv_exchange"):
-        by_head = lambda a: a[0].reshape(tok, n_row, HEAD_DIM).transpose(1, 0, 2)
-        stacked = jnp.stack([by_head(queries), by_head(keys_in), by_head(values_in)], axis=1)
-        heads = lax.all_to_all(stacked, ROW, 0, 0, tiled=True)
-        query, key, value = (heads[:, i].reshape(seq_len, HEAD_DIM) for i in range(3))
+        query, key, value = spread_heads([queries[0], keys_in[0], values_in[0]])
 
     with jax.named_scope("weight_swap"):
         w_rows = out_weight.reshape(-1, width)
@@ -92,7 +158,7 @@
         w1 = jnp.where(first, w_other, w_own)
 
     with jax.named_scope("attend"):
-        head_out, probs = attention_forward(query, key, value)
+        head_out = attention_forward(query, key, value)
 
     with jax.named_scope("head_gather"):
         x_index = lax.axis_index("x")
@@ -105,41 +171,43 @@
     with jax.named_scope("project"):
         part0 = jnp.dot(heads_x, w0, preferred_element_type=F32).astype(BF16)
         part1 = jnp.dot(heads_x, w1, preferred_element_type=F32).astype(BF16)
-        part0, part1, grad_all = lax.optimization_barrier((part0, part1, grad_all))
         parts = jnp.concatenate([part0, part1], axis=0)
         parts, grad_all = lax.optimization_barrier((parts, grad_all))
         projected = lax.psum_scatter(parts, RING, scatter_dimension=0, tiled=True)
+
+    with jax.named_scope("weight_grad"):
+        over_t = (((0,), (0,)), ((), ()))
+        dw = [
+            lax.dot_general(heads_x, grad_all[i], over_t, preferred_element_type=F32).astype(BF16) for i in range(2)
+        ]
+        *dw, grad_all = lax.optimization_barrier((*dw, grad_all))
 
     with jax.named_scope("head_grad"):
         over_n = (((1,), (1,)), ((), ()))
         hg = lax.dot_general(grad_all[0], w0, over_n, preferred_element_type=F32)
         hg = hg + lax.dot_general(grad_all[1], w1, over_n, preferred_element_type=F32)
         hg = hg.astype(BF16).reshape(seq_len, n_x, HEAD_DIM).transpose(1, 0, 2)
-        hg = lax.all_to_all(hg, "x", 0, 0, tiled=True)
-        grad = jnp.sum(hg.astype(F32), axis=0).astype(BF16)
+        grad_parts = lax.all_to_all(hg, "x", 0, 0, tiled=True)
 
     with jax.named_scope("weight_grad"):
-        over_t = (((0,), (0,)), ((), ()))
-        dw = [
-            lax.dot_general(heads_x, grad_all[i], over_t, preferred_element_type=F32).astype(BF16) for i in range(2)
-        ]
         dw = reduce_scatter_dp(dw, piece)
         dw_own = lax.dynamic_index_in_dim(dw, zhi, 0, keepdims=False)
         dw_away = lax.dynamic_index_in_dim(dw, 1 - zhi, 0, keepdims=False)
         dw_back = lax.ppermute(dw_away, "zhi", swap)
+    with jax.named_scope("attend_back"):
+        back = attention_backward(query, key, value, grad_parts, tok)
+
+    with jax.named_scope("qkv_return"):
+        back, dw_back = lax.optimization_barrier((back, dw_back))
+        back = lax.all_to_all(back, ROW, 0, 0, tiled=True)
+        outs = [back[:, i].transpose(1, 0, 2).reshape(1, tok, n_row * HEAD_DIM) for i in range(3)]
+    with jax.named_scope("weight_grad"):
         own_rows = lax.all_gather(dw_own, DP, axis=0, tiled=True)
         other_rows = lax.all_gather(dw_back, DP, axis=0, tiled=True)
         grad_weight = jnp.concatenate(
             [jnp.where(first, own_rows, other_rows), jnp.where(first, other_rows, own_rows)], axis=0
         ).reshape(out_weight.shape)
 
-    with jax.named_scope("attend_back"):
-        grads = attention_backward(query, key, value, probs, grad)
-
-    with jax.named_scope("qkv_return"):
-        back = jnp.stack([g.reshape(n_row, tok, HEAD_DIM) for g in grads], axis=1)
-        back = lax.all_to_all(back, ROW, 0, 0, tiled=True)
-        outs = [back[:, i].transpose(1, 0, 2).reshape(1, tok, n_row * HEAD_DIM) for i in range(3)]
     return (projected[None], *outs, grad_weight)
 
 

time: 240 us -> 234 us (0.975)
  the two profiles are of different devices: /device:TPU:12 before, /device:TPU:4 now
where the time goes in v4:
time: 234 us; the launch traced here: 233 us
  starting transfers between devices  81 us (35%)
  waiting for transfers between devices  64.7 us (28%)
  blocking collectives  40.8 us (17%)
  between operations  14.9 us (6%)
  matrix products  11.1 us (5%)
  local copies, waits for them, and re-layouts  9.96 us (4%)
  other arithmetic  6.56 us (3%)
  Pallas kernels  4.33 us (2%)
    ppermute x7, starting transfers between devices, spread_heads(): lax.ppermute(cut((row + d) % n_row), 'row', pairs)  26.5 us
    all_gather x1, waiting for transfers between devices, body(): lax.all_gather(out_grad[0], RING, axis=0, tiled=True)  20.3 us
    all_to_all x1, waiting for transfers between devices, body(): back = lax.all_to_all(back, ROW, 0, 0, tiled=True)  18.1 us
    ppermute x1, starting transfers between devices, body(): arrived = lax.ppermute(away, 'zhi', swap)  15.7 us
    all_gather x1, blocking collectives, body(): w_other = lax.all_gather(arrived, DP, axis=0, tiled=True)  13.9 us
    all_gather x1, blocking collectives, body(): own_rows = lax.all_gather(dw_own, DP, axis=0, tiled=True)  13.5 us
    all_gather x1, blocking collectives, body(): other_rows = lax.all_gather(dw_back, DP, axis=0, tiled=True)  13.5 us
    ppermute x7, waiting for transfers between devices, spread_heads(): lax.ppermute(cut((row + d) % n_row), 'row', pairs)  11.7 us
  transfers between devices with their start and end apart: 20, of which 10 were waited for; matrix products, arithmetic and copies ran while one was open for 11% of the time, Pallas kernels for 2%

profile of v4, /device:TPU:4, one launch (start us, length us, event | category | flops | bytes accessed | tf_op | source)
XLA Modules:
  0.0 233.4 jit_solution(4465103169972150923)
XLA Ops:
  8.9 15.7 %collective-permute-start.10 = (bf16[64,768]{1,0:T(8,128)(2,1)S(1)}, bf16[64,768]{1,0:T(8,128)(2,1)S(1)}, u32[]{:S(2)}, u32[]{:S(2)}) collective-permute-start(bf16[64,768]{1,0:T(8,128)(2,1)S(1)} %constant_dynamic-slice_fusion.1), channel_id=1, source_target_pairs={{0,4},{4,0},{1,5},{5,1},{2,6},{6,2},{3,7},{7,3},{8,12},{12,8},{9,1... | collective-permute-start | bytes 294920 | tf_op jit(solution)/shard_map/weight_swap/ppermute | solution.py:153
  26.7 2.9 %collective-permute-start = (bf16[3,128,128]{2,1,0:T(8,128)(2,1)S(1)}, bf16[3,128,128]{2,1,0:T(8,128)(2,1)S(1)}, u32[]{:S(2)}, u32[]{:S(2)}) collective-permute-start(bf16[3,128,128]{2,1,0:T(8,128)(2,1)S(1)} %pad_maximum_fusion.4), channel_id=1, source_target_pairs={{0,8},{8,16},{16,24},{24,32},{32,40},{40,48},{48,56},{56,0},{1,9},... | collective-permute-start | bytes 294920 | tf_op jit(solution)/shard_map/qkv_exchange/ppermute | solution.py:96
  29.7 3.4 %collective-permute-start.1 = (bf16[3,128,128]{2,1,0:T(8,128)(2,1)S(1)}, bf16[3,128,128]{2,1,0:T(8,128)(2,1)S(1)}, u32[]{:S(2)}, u32[]{:S(2)}) collective-permute-start(bf16[3,128,128]{2,1,0:T(8,128)(2,1)S(1)} %pad_maximum_fusion.5), channel_id=1, source_target_pairs={{0,16},{8,24},{16,32},{24,40},{32,48},{40,56},{48,0},{56,8},{1,17}... | collective-permute-start | bytes 294920 | tf_op jit(solution)/shard_map/qkv_exchange/ppermute | solution.py:96
  33.1 3.8 %collective-permute-start.2 = (bf16[3,128,128]{2,1,0:T(8,128)(2,1)S(1)}, bf16[3,128,128]{2,1,0:T(8,128)(2,1)S(1)}, u32[]{:S(2)}, u32[]{:S(2)}) collective-permute-start(bf16[3,128,128]{2,1,0:T(8,128)(2,1)S(1)} %pad_maximum_fusion.6), channel_id=1, source_target_pairs={{0,24},{8,32},{16,40},{24,48},{32,56},{40,0},{48,8},{56,16},{1,25}... | collective-permute-start | bytes 294920 | tf_op jit(solution)/shard_map/qkv_exchange/ppermute | solution.py:96
  36.9 7.3 %collective-permute-start.3 = (bf16[3,128,128]{2,1,0:T(8,128)(2,1)S(1)}, bf16[3,128,128]{2,1,0:T(8,128)(2,1)S(1)}, u32[]{:S(2)}, u32[]{:S(2)}) collective-permute-start(bf16[3,128,128]{2,1,0:T(8,128)(2,1)S(1)} %pad_maximum_fusion.7), channel_id=1, source_target_pairs={{0,32},{8,40},{16,48},{24,56},{32,0},{40,8},{48,16},{56,24},{1,33}... | collective-permute-start | bytes 294920 | tf_op jit(solution)/shard_map/qkv_exchange/ppermute | solution.py:96
  44.6 3.0 %collective-permute-start.4 = (bf16[3,128,128]{2,1,0:T(8,128)(2,1)S(1)}, bf16[3,128,128]{2,1,0:T(8,128)(2,1)S(1)}, u32[]{:S(2)}, u32[]{:S(2)}) collective-permute-start(bf16[3,128,128]{2,1,0:T(8,128)(2,1)S(1)} %pad_maximum_fusion.8), channel_id=1, source_target_pairs={{0,40},{8,48},{16,56},{24,0},{32,8},{40,16},{48,24},{56,32},{1,41}... | collective-permute-start | bytes 294920 | tf_op jit(solution)/shard_map/qkv_exchange/ppermute | solution.py:96
  49.8 4.2 %collective-permute-start.5 = (bf16[3,128,128]{2,1,0:T(8,128)(2,1)S(1)}, bf16[3,128,128]{2,1,0:T(8,128)(2,1)S(1)}, u32[]{:S(2)}, u32[]{:S(2)}) collective-permute-start(bf16[3,128,128]{2,1,0:T(8,128)(2,1)S(1)} %pad_maximum_fusion.9), channel_id=1, source_target_pairs={{0,48},{8,56},{16,0},{24,8},{32,16},{40,24},{48,32},{56,40},{1,49}... | collective-permute-start | bytes 294920 | tf_op jit(solution)/shard_map/qkv_exchange/ppermute | solution.py:96
  54.0 3.3 %collective-permute-done.2 = bf16[3,128,128]{2,1,0:T(8,128)(2,1)S(1)} collective-permute-done((bf16[3,128,128]{2,1,0:T(8,128)(2,1)S(1)}, bf16[3,128,128]{2,1,0:T(8,128)(2,1)S(1)}, u32[]{:S(2)}, u32[]{:S(2)}) %collective-permute-start.2) | collective-permute-done | bytes 98336 | tf_op jit(solution)/shard_map/qkv_exchange/ppermute | solution.py:96
  60.7 3.8 %collective-permute-done.5 = bf16[3,128,128]{2,1,0:T(8,128)(2,1)S(1)} collective-permute-done((bf16[3,128,128]{2,1,0:T(8,128)(2,1)S(1)}, bf16[3,128,128]{2,1,0:T(8,128)(2,1)S(1)}, u32[]{:S(2)}, u32[]{:S(2)}) %collective-permute-start.5) | collective-permute-done | bytes 98336 | tf_op jit(solution)/shard_map/qkv_exchange/ppermute | solution.py:96
  67.6 2.5 %collective-permute-start.9 = (bf16[1024,128]{0,1:T(8,128)(2,1)S(1)}, bf16[1024,128]{0,1:T(8,128)(2,1)S(1)}, u32[]{:S(2)}, u32[]{:S(2)}) collective-permute-start(bf16[1024,128]{0,1:T(8,128)(2,1)S(1)} %fusion.21), channel_id=1, source_target_pairs={{0,3},{1,0},{2,1},{3,2},{4,7},{5,4},{6,5},{7,6},{8,11},{9,8},{10,9... | collective-permute-start | bytes 786440 | tf_op jit(solution)/shard_map/head_gather/ppermute | solution.py:165
  70.1 4.5 %collective-permute-start.8 = (bf16[1024,128]{0,1:T(8,128)(2,1)S(1)}, bf16[1024,128]{0,1:T(8,128)(2,1)S(1)}, u32[]{:S(2)}, u32[]{:S(2)}) collective-permute-start(bf16[1024,128]{0,1:T(8,128)(2,1)S(1)} %fusion.21), channel_id=1, source_target_pairs={{0,2},{1,3},{2,0},{3,1},{4,6},{5,7},{6,4},{7,5},{8,10},{9,11},{10,... | collective-permute-start | bytes 786440 | tf_op jit(solution)/shard_map/head_gather/ppermute | solution.py:165
  76.6 13.9 %all_gather.12 = bf16[512,768]{1,0:T(8,128)(2,1)S(1)} all-gather(bf16[64,768]{1,0:T(8,128)(2,1)S(1)} %collective-permute-done.10), channel_id=1, replica_groups=mesh['y'=4,'core'=2,'row'=8,'zhi'=2,'x'=4] {'y','core'}, dimensions={0}, use_global_device_ids=true | all-gather | bytes 884736 | tf_op jit(solution)/shard_map/weight_swap/all_gather | solution.py:154
  96.2 20.3 %all-gather.4.cloned.1.call-done = bf16[1,2048,768]{2,1,0:T(8,128)(2,1)} async-done(((bf16[1,128,768]{2,1,0:T(8,128)(2,1)}), bf16[1,2048,768]{2,1,0:T(8,128)(2,1)}) %all-gather.4.cloned.1.call-update) | async-done | bytes 3145744 | tf_op jit(solution)/shard_map/grad_gather/all_gather | solution.py:143
  122.1 3.0 %fusion.4 = f32[1024,512]{0,1:T(8,128)S(1)} fusion(bf16[2,1024,768]{2,1,0:T(8,128)(2,1)} %bitcast.104, bf16[512,768]{1,0:T(8,128)(2,1)} %copy-done, pred[]{:T(512)S(6)} %eq.25, bf16[1024,768]{1,0:T(8,128)(2,1)} %bitcast.99, s32[]{:T(128)S(6)} %select_n.258), kind=kOutput, calls=%fused_computation.18 | convolution fusion | flops 805699584 | bytes 5242885 | tf_op jit(solution)/shard_map/head_grad/dot_general | solution.py:188
  127.4 5.2 %collective-permute-start.14 = (bf16[2,64,768]{2,1,0:T(8,128)(2,1)}, bf16[2,64,768]{2,1,0:T(8,128)(2,1)S(1)}, u32[]{:S(2)}, u32[]{:S(2)}) collective-permute-start(bf16[2,64,768]{2,1,0:T(8,128)(2,1)} %get-tuple-element.34), channel_id=1, source_target_pairs={{0,384},{128,0},{256,128},{384,256},{1,385},{129,1},{257,129},{385... | collective-permute-start | bytes 589832 | tf_op jit(solution)/shard_map/weight_grad/ppermute | solution.py:127
  135.1 2.8 %collective-permute-start.12 = (bf16[2,64,768]{2,1,0:T(8,128)(2,1)S(1)}, bf16[2,64,768]{2,1,0:T(8,128)(2,1)}, u32[]{:S(2)}, u32[]{:S(2)}) collective-permute-start(bf16[2,64,768]{2,1,0:T(8,128)(2,1)S(1)} %get-tuple-element.33), channel_id=1, source_target_pairs={{0,128},{128,256},{256,384},{384,0},{1,129},{129,257},{257,385},{3... | collective-permute-start | bytes 589832 | tf_op jit(solution)/shard_map/weight_grad/ppermute | solution.py:127
  140.3 4.8 %all-to-all-start = ((bf16[4,1024,128]{2,1,0:T(8,128)(2,1)}), bf16[4,1024,128]{2,1,0:T(8,128)(2,1)S(1)}, u32[]{:S(2)}, u32[]{:S(2)}) async-start(bf16[4,1024,128]{2,1,0:T(8,128)(2,1)} %bitcast.19), calls=%async_computation.1 | async-start | bytes 2097152 | tf_op jit(solution)/shard_map/head_grad/all_to_all | solution.py:190
  148.4 7.3 %collective-permute-start.15 = (bf16[64,768]{1,0:T(8,128)(2,1)S(1)}, bf16[64,768]{1,0:T(8,128)(2,1)S(1)}, u32[]{:S(2)}, u32[]{:S(2)}) collective-permute-start(bf16[64,768]{1,0:T(8,128)(2,1)S(1)} %get-tuple-element.64), channel_id=1, source_target_pairs={{0,4},{4,0},{1,5},{5,1},{2,6},{6,2},{3,7},{7,3},{8,12},{12,8},{9,1... | collective-permute-start | bytes 294920 | tf_op jit(solution)/shard_map/weight_grad/ppermute | solution.py:196
  157.0 4.3 %attend_back.1 = bf16[8,3,128,128]{3,2,1,0:T(8,128)(2,1)} custom-call(bf16[1024,128]{1,0:T(8,128)(2,1)S(1)} %get-tuple-element.38.query_ref, bf16[1024,128]{1,0:T(8,128)(2,1)S(1)} %get-tuple-element.37.key_ref, bf16[1024,128]{1,0:T(8,128)(2,1)S(1)} %get-tuple-element.36.value_ref, bf16[4,1024,128]{2,1,0:T(8,128)(2,1)S(1)} %all-to-all-done.parts_ref), custom_call_target="tpu_custom_call" | custom-call | flops 939524096 | bytes 2097152 | tf_op jit(solution)/shard_map/attend_back/pallas_call | solution.py:73
  161.4 10.4 %collective-permute-done.15 = bf16[64,768]{1,0:T(8,128)(2,1)S(1)} collective-permute-done((bf16[64,768]{1,0:T(8,128)(2,1)S(1)}, bf16[64,768]{1,0:T(8,128)(2,1)S(1)}, u32[]{:S(2)}, u32[]{:S(2)}) %collective-permute-start.15) | collective-permute-done | bytes 98336 | tf_op jit(solution)/shard_map/weight_grad/ppermute | solution.py:196
  171.8 5.3 %all-to-all-start.1 = ((bf16[8,3,128,128]{3,2,1,0:T(8,128)(2,1)}), bf16[8,3,128,128]{3,2,1,0:T(8,128)(2,1)S(1)}, u32[]{:S(2)}, u32[]{:S(2)}) async-start(bf16[8,3,128,128]{3,2,1,0:T(8,128)(2,1)} %attend_back.1), calls=%async_computation.2 | async-start | bytes 1572864 | tf_op jit(solution)/shard_map/qkv_return/all_to_all | solution.py:202
  177.0 13.5 %all-gather.1 = bf16[1,512,768]{2,1,0:T(8,128)(2,1)S(1)} all-gather(bf16[1,64,768]{2,1,0:T(8,128)(2,1)S(1)} %get-tuple-element.63), channel_id=3, replica_groups=mesh['y'=4,'core'=2,'row'=8,'zhi'=2,'x'=4] {'y','core'}, dimensions={1}, use_global_device_ids=true | all-gather | bytes 884736 | tf_op jit(solution)/shard_map/weight_grad/all_gather | solution.py:205
  190.5 13.5 %all_gather.15 = bf16[512,768]{1,0:T(8,128)(2,1)S(1)} all-gather(bf16[64,768]{1,0:T(8,128)(2,1)S(1)} %collective-permute-done.15), channel_id=1, replica_groups=mesh['y'=4,'core'=2,'row'=8,'zhi'=2,'x'=4] {'y','core'}, dimensions={0}, use_global_device_ids=true | all-gather | bytes 884736 | tf_op jit(solution)/shard_map/weight_grad/all_gather | solution.py:206
  205.3 18.1 %all-to-all-done.1 = bf16[8,3,128,128]{3,2,1,0:T(8,128)(2,1)S(1)} async-done(((bf16[8,3,128,128]{3,2,1,0:T(8,128)(2,1)}), bf16[8,3,128,128]{3,2,1,0:T(8,128)(2,1)S(1)}, u32[]{:S(2)}, u32[]{:S(2)}) %all-to-all-start.1) | async-done | bytes 786464 | tf_op jit(solution)/shard_map/qkv_return/all_to_all | solution.py:202
  (81 shorter events, 41.8 us)
Async XLA Ops:
  7.2 109.3 %all-gather.4.cloned.1.call-start = ((), (), s32[]{:S(2)}) async-start(), calls=%async_computation.4 | async-start | bytes 3342336 | tf_op jit(solution)/shard_map/grad_gather/all_gather | solution.py:143
  7.9 218.7 %reduce-scatter.2.cloned.1.call-start = ((), (), s32[]{:S(2)}) async-start(), calls=%async_computation.3 | async-start | bytes 3342336 | tf_op jit(solution)/shard_map/project/reduce_scatter | solution.py:176
  8.9 67.7 %collective-permute-start.10 = (bf16[64,768]{1,0:T(8,128)(2,1)S(1)}, bf16[64,768]{1,0:T(8,128)(2,1)S(1)}, u32[]{:S(2)}, u32[]{:S(2)}) collective-permute-start(bf16[64,768]{1,0:T(8,128)(2,1)S(1)} %constant_dynamic-slice_fusion.1), channel_id=1, source_target_pairs={{0,4},{4,0},{1,5},{5,1},{2,6},{6,2},{3,7},{7,3},{8,12},{12,8},{9,1... | collective-permute-start | bytes 294920 | tf_op jit(solution)/shard_map/weight_swap/ppermute | solution.py:153
  26.7 17.9 %collective-permute-start = (bf16[3,128,128]{2,1,0:T(8,128)(2,1)S(1)}, bf16[3,128,128]{2,1,0:T(8,128)(2,1)S(1)}, u32[]{:S(2)}, u32[]{:S(2)}) collective-permute-start(bf16[3,128,128]{2,1,0:T(8,128)(2,1)S(1)} %pad_maximum_fusion.4), channel_id=1, source_target_pairs={{0,8},{8,16},{16,24},{24,32},{32,40},{40,48},{48,56},{56,0},{1,9},... | collective-permute-start | bytes 294920 | tf_op jit(solution)/shard_map/qkv_exchange/ppermute | solution.py:96
  29.7 20.2 %collective-permute-start.1 = (bf16[3,128,128]{2,1,0:T(8,128)(2,1)S(1)}, bf16[3,128,128]{2,1,0:T(8,128)(2,1)S(1)}, u32[]{:S(2)}, u32[]{:S(2)}) collective-permute-start(bf16[3,128,128]{2,1,0:T(8,128)(2,1)S(1)} %pad_maximum_fusion.5), channel_id=1, source_target_pairs={{0,16},{8,24},{16,32},{24,40},{32,48},{40,56},{48,0},{56,8},{1,17}... | collective-permute-start | bytes 294920 | tf_op jit(solution)/shard_map/qkv_exchange/ppermute | solution.py:96
  33.1 24.3 %collective-permute-start.2 = (bf16[3,128,128]{2,1,0:T(8,128)(2,1)S(1)}, bf16[3,128,128]{2,1,0:T(8,128)(2,1)S(1)}, u32[]{:S(2)}, u32[]{:S(2)}) collective-permute-start(bf16[3,128,128]{2,1,0:T(8,128)(2,1)S(1)} %pad_maximum_fusion.6), channel_id=1, source_target_pairs={{0,24},{8,32},{16,40},{24,48},{32,56},{40,0},{48,8},{56,16},{1,25}... | collective-permute-start | bytes 294920 | tf_op jit(solution)/shard_map/qkv_exchange/ppermute | solution.py:96
  36.9 22.4 %collective-permute-start.3 = (bf16[3,128,128]{2,1,0:T(8,128)(2,1)S(1)}, bf16[3,128,128]{2,1,0:T(8,128)(2,1)S(1)}, u32[]{:S(2)}, u32[]{:S(2)}) collective-permute-start(bf16[3,128,128]{2,1,0:T(8,128)(2,1)S(1)} %pad_maximum_fusion.7), channel_id=1, source_target_pairs={{0,32},{8,40},{16,48},{24,56},{32,0},{40,8},{48,16},{56,24},{1,33}... | collective-permute-start | bytes 294920 | tf_op jit(solution)/shard_map/qkv_exchange/ppermute | solution.py:96
  44.6 16.0 %collective-permute-start.4 = (bf16[3,128,128]{2,1,0:T(8,128)(2,1)S(1)}, bf16[3,128,128]{2,1,0:T(8,128)(2,1)S(1)}, u32[]{:S(2)}, u32[]{:S(2)}) collective-permute-start(bf16[3,128,128]{2,1,0:T(8,128)(2,1)S(1)} %pad_maximum_fusion.8), channel_id=1, source_target_pairs={{0,40},{8,48},{16,56},{24,0},{32,8},{40,16},{48,24},{56,32},{1,41}... | collective-permute-start | bytes 294920 | tf_op jit(solution)/shard_map/qkv_exchange/ppermute | solution.py:96
  49.8 14.6 %collective-permute-start.5 = (bf16[3,128,128]{2,1,0:T(8,128)(2,1)S(1)}, bf16[3,128,128]{2,1,0:T(8,128)(2,1)S(1)}, u32[]{:S(2)}, u32[]{:S(2)}) collective-permute-start(bf16[3,128,128]{2,1,0:T(8,128)(2,1)S(1)} %pad_maximum_fusion.9), channel_id=1, source_target_pairs={{0,48},{8,56},{16,0},{24,8},{32,16},{40,24},{48,32},{56,40},{1,49}... | collective-permute-start | bytes 294920 | tf_op jit(solution)/shard_map/qkv_exchange/ppermute | solution.py:96
  57.3 8.2 %collective-permute-start.6 = (bf16[3,128,128]{2,1,0:T(8,128)(2,1)S(1)}, bf16[3,128,128]{2,1,0:T(8,128)(2,1)S(1)}, u32[]{:S(2)}, u32[]{:S(2)}) collective-permute-start(bf16[3,128,128]{2,1,0:T(8,128)(2,1)S(1)} %pad_maximum_fusion.10), channel_id=1, source_target_pairs={{0,56},{8,0},{16,8},{24,16},{32,24},{40,32},{48,40},{56,48},{1,57}... | collective-permute-start | bytes 294920 | tf_op jit(solution)/shard_map/qkv_exchange/ppermute | solution.py:96
  67.6 22.9 %collective-permute-start.9 = (bf16[1024,128]{0,1:T(8,128)(2,1)S(1)}, bf16[1024,128]{0,1:T(8,128)(2,1)S(1)}, u32[]{:S(2)}, u32[]{:S(2)}) collective-permute-start(bf16[1024,128]{0,1:T(8,128)(2,1)S(1)} %fusion.21), channel_id=1, source_target_pairs={{0,3},{1,0},{2,1},{3,2},{4,7},{5,4},{6,5},{7,6},{8,11},{9,8},{10,9... | collective-permute-start | bytes 786440 | tf_op jit(solution)/shard_map/head_gather/ppermute | solution.py:165
  70.1 20.4 %collective-permute-start.8 = (bf16[1024,128]{0,1:T(8,128)(2,1)S(1)}, bf16[1024,128]{0,1:T(8,128)(2,1)S(1)}, u32[]{:S(2)}, u32[]{:S(2)}) collective-permute-start(bf16[1024,128]{0,1:T(8,128)(2,1)S(1)} %fusion.21), channel_id=1, source_target_pairs={{0,2},{1,3},{2,0},{3,1},{4,6},{5,7},{6,4},{7,5},{8,10},{9,11},{10,... | collective-permute-start | bytes 786440 | tf_op jit(solution)/shard_map/head_gather/ppermute | solution.py:165
  74.6 15.9 %collective-permute-start.7 = (bf16[1024,128]{0,1:T(8,128)(2,1)S(1)}, bf16[1024,128]{0,1:T(8,128)(2,1)S(1)}, u32[]{:S(2)}, u32[]{:S(2)}) collective-permute-start(bf16[1024,128]{0,1:T(8,128)(2,1)S(1)} %fusion.21), channel_id=1, source_target_pairs={{0,1},{1,2},{2,3},{3,0},{4,5},{5,6},{6,7},{7,4},{8,9},{9,10},{10,1... | collective-permute-start | bytes 786440 | tf_op jit(solution)/shard_map/head_gather/ppermute | solution.py:165
  90.5 2.8 %copy-start = (bf16[512,768]{1,0:T(8,128)(2,1)}, bf16[512,768]{1,0:T(8,128)(2,1)S(1)}, u32[]{:S(2)}) copy-start(bf16[512,768]{1,0:T(8,128)(2,1)S(1)} %all_gather.12) | copy-start | bytes 2359300
  120.1 5.0 %collective-permute-start.11 = (bf16[4,2,64,768]{3,2,0,1:T(8,128)(2,1)S(1)}, bf16[4,2,64,768]{3,2,0,1:T(8,128)(2,1)}, u32[]{:S(2)}, u32[]{:S(2)}) collective-permute-start(bf16[4,2,64,768]{3,2,0,1:T(8,128)(2,1)S(1)} %fusion.23), channel_id=1, source_target_pairs={{0,64},{64,0},{1,65},{65,1},{2,66},{66,2},{3,67},{67,3},{4,68},{68... | collective-permute-start | bytes 2359304 | tf_op jit(solution)/shard_map/weight_grad/ppermute | solution.py:123
  122.1 15.8 %copy-start.5 = (bf16[1,2048,768]{2,1,0:T(8,128)(2,1)S(1)}, bf16[1,2048,768]{2,1,0:T(8,128)(2,1)}, u32[]{:S(2)}) copy-start(bf16[1,2048,768]{2,1,0:T(8,128)(2,1)} %all-gather.4.cloned.1.call-done) | copy-start | bytes 9437188
  125.1 12.8 %copy-start.1 = (bf16[512,768]{1,0:T(8,128)(2,1)S(1)}, bf16[512,768]{1,0:T(8,128)(2,1)}, u32[]{:S(2)}) copy-start(bf16[512,768]{1,0:T(8,128)(2,1)} %copy-done) | copy-start | bytes 2359300
  125.1 12.8 %copy-start.3 = (bf16[8,1,128,768]{3,2,1,0:T(8,128)(2,1)S(1)}, bf16[8,1,128,768]{3,2,1,0:T(8,128)(2,1)}, u32[]{:S(2)}) copy-start(bf16[8,1,128,768]{3,2,1,0:T(8,128)(2,1)} %param.8) | copy-start | bytes 4718596
  127.4 17.7 %collective-permute-start.14 = (bf16[2,64,768]{2,1,0:T(8,128)(2,1)}, bf16[2,64,768]{2,1,0:T(8,128)(2,1)S(1)}, u32[]{:S(2)}, u32[]{:S(2)}) collective-permute-start(bf16[2,64,768]{2,1,0:T(8,128)(2,1)} %get-tuple-element.34), channel_id=1, source_target_pairs={{0,384},{128,0},{256,128},{384,256},{1,385},{129,1},{257,129},{385... | collective-permute-start | bytes 589832 | tf_op jit(solution)/shard_map/weight_grad/ppermute | solution.py:127
  132.6 12.5 %collective-permute-start.13 = (bf16[2,64,768]{2,1,0:T(8,128)(2,1)S(1)}, bf16[2,64,768]{2,1,0:T(8,128)(2,1)S(1)}, u32[]{:S(2)}, u32[]{:S(2)}) collective-permute-start(bf16[2,64,768]{2,1,0:T(8,128)(2,1)S(1)} %get-tuple-element.35), channel_id=1, source_target_pairs={{0,256},{128,384},{256,0},{384,128},{1,257},{129,385},{257,1},{385... | collective-permute-start | bytes 589832 | tf_op jit(solution)/shard_map/weight_grad/ppermute | solution.py:127
  135.1 12.2 %collective-permute-start.12 = (bf16[2,64,768]{2,1,0:T(8,128)(2,1)S(1)}, bf16[2,64,768]{2,1,0:T(8,128)(2,1)}, u32[]{:S(2)}, u32[]{:S(2)}) collective-permute-start(bf16[2,64,768]{2,1,0:T(8,128)(2,1)S(1)} %get-tuple-element.33), channel_id=1, source_target_pairs={{0,128},{128,256},{256,384},{384,0},{1,129},{129,257},{257,385},{3... | collective-permute-start | bytes 589832 | tf_op jit(solution)/shard_map/weight_grad/ppermute | solution.py:127
  140.3 16.7 %all-to-all-start = ((bf16[4,1024,128]{2,1,0:T(8,128)(2,1)}), bf16[4,1024,128]{2,1,0:T(8,128)(2,1)S(1)}, u32[]{:S(2)}, u32[]{:S(2)}) async-start(bf16[4,1024,128]{2,1,0:T(8,128)(2,1)} %bitcast.19), calls=%async_computation.1 | async-start | bytes 2097152 | tf_op jit(solution)/shard_map/head_grad/all_to_all | solution.py:190
  148.4 23.4 %collective-permute-start.15 = (bf16[64,768]{1,0:T(8,128)(2,1)S(1)}, bf16[64,768]{1,0:T(8,128)(2,1)S(1)}, u32[]{:S(2)}, u32[]{:S(2)}) collective-permute-start(bf16[64,768]{1,0:T(8,128)(2,1)S(1)} %get-tuple-element.64), channel_id=1, source_target_pairs={{0,4},{4,0},{1,5},{5,1},{2,6},{6,2},{3,7},{7,3},{8,12},{12,8},{9,1... | collective-permute-start | bytes 294920 | tf_op jit(solution)/shard_map/weight_grad/ppermute | solution.py:196
  171.8 51.6 %all-to-all-start.1 = ((bf16[8,3,128,128]{3,2,1,0:T(8,128)(2,1)}), bf16[8,3,128,128]{3,2,1,0:T(8,128)(2,1)S(1)}, u32[]{:S(2)}, u32[]{:S(2)}) async-start(bf16[8,3,128,128]{3,2,1,0:T(8,128)(2,1)} %attend_back.1), calls=%async_computation.2 | async-start | bytes 1572864 | tf_op jit(solution)/shard_map/qkv_return/all_to_all | solution.py:202
  (2 other events, 4.2 us)
Sparse Core Ops, SparseCore 0:
  10.1 106.3 all-gather.3
  119.9 99.8 reduce-scatter.1
